TPU v7x, 128 devices: a whole 4x4x4 slice. The times are simulated.
128 devices in a mesh: seq: 64 (over z, x, y), head: 2 (over core).
Axes of the slice: x: 4, y: 4, z: 4, core: 2. Of those that a mesh axis runs over, the one named last changes fastest.
Arguments:
- queries: bfloat16 [8192, 32, 128], P('seq', 'head'), may hold values from -240 to 240
- keys: bfloat16 [8192, 32, 128], P('seq', 'head'), may hold values from -6 to 6
- values: bfloat16 [8192, 32, 128], P('seq', 'head'), may hold values from -6 to 6
- target: bfloat16 [8192, 32, 128], P('seq', 'head'), may hold values from -6 to 6
- map_q: bfloat16 [128, 64], replicated, may hold values from -0.5 to 0.5
- map_k: bfloat16 [128, 64], replicated, may hold values from -0.5 to 0.5
Outputs:
- hybrid: bfloat16 [8192, 32, 128], P('seq', 'head')
- grad_q: float32 [128, 64], replicated
- grad_k: float32 [128, 64], replicated
All inputs are finite; a program needn't handle non-finite values.
Results may differ from a plain program's by a relative error of at most 0.001.
The roundings to bfloat16 on the way count: a program that leaves them out, or rounds other values in their place, can miss the bound.
Values may be sent and summed in bfloat16 or wider, within the bound.
A program may use at most 192 MiB of HBM per device.

v0:
```python
import jax
import jax.numpy as jnp
from jax import lax
from jax.sharding import PartitionSpec as P

WINDOW = 64


state_precision = lax.Precision.HIGH


def from_behind(value, axis, steps):
    count = lax.axis_size(axis)
    initial, last = (max(0, -steps), min(count, count - steps))
    return lax.ppermute(value, axis, [(source, source + steps) for source in range(initial, last)])


def prefix(array, axis, combine, identity, reverse):
    count, here = (lax.axis_size(axis), lax.axis_index(axis))
    everything = jax.tree.map(lambda part: lax.all_gather(part, axis), array)
    start = jax.tree.map(
        lambda part, zero: jnp.broadcast_to(jnp.asarray(zero, part.dtype), part.shape),
        array,
        identity,
    )

    def turn(k, before):
        at = count - 1 - k if reverse else k
        reached = at > here if reverse else at < here
        new = combine(before, jax.tree.map(lambda part: part[at], everything))
        return jax.tree.map(lambda a, b: jnp.where(reached, a, b), new, before)

    return lax.fori_loop(0, count, turn, start)


def feature_map(inputs, weight):
    hidden = jnp.einsum("thd,df->thf", inputs, weight, preferred_element_type=jnp.float32)
    upper_soft = jax.nn.softmax(hidden, axis=-1)
    lower_soft = jax.nn.softmax(-hidden, axis=-1)
    return (
        jnp.concatenate([upper_soft, lower_soft], -1).astype(jnp.bfloat16),
        upper_soft,
        lower_soft,
    )


def feature_grad(inputs, upper_soft, lower_soft, upstream):
    feat_width = upper_soft.shape[-1]
    upper_grad = upstream[..., :feat_width]
    lower_grad = upstream[..., feat_width:]
    inner_grad = upper_soft * (upper_grad - jnp.sum(upper_grad * upper_soft, -1, keepdims=True))
    inner_grad = inner_grad - lower_soft * (
        lower_grad - jnp.sum(lower_grad * lower_soft, -1, keepdims=True)
    )
    return jnp.einsum(
        "thd,thf->df", inputs, inner_grad.astype(jnp.bfloat16), preferred_element_type=jnp.float32
    )


def add_pair(earlier_part, later_part):
    return (earlier_part[0] + later_part[0], earlier_part[1] + later_part[1])


def per_device(queries, keys, values, target, map_q, map_k):
    tok_rows, head_local, head_size = queries.shape
    window = WINDOW
    blocks = tok_rows // window
    seq_count = lax.axis_size("seq")
    device_pos = lax.axis_index("seq")
    score_scale = head_size ** (-0.5)
    total_tokens = tok_rows * seq_count
    has_prior = device_pos > 0
    phi_q, q_upper, q_lower = feature_map(queries, map_q)
    phi_k, k_upper, k_lower = feature_map(keys, map_k)
    edge_start = tok_rows - window
    halo_keys, halo_values = from_behind((keys[edge_start:], values[edge_start:]), "seq", 1)
    halo_phi, halo_upper, halo_lower = feature_map(halo_keys, map_k)
    halo_phi = jnp.where(has_prior, halo_phi, jnp.zeros_like(halo_phi))
    feat_all = phi_k.shape[-1]
    ext_keys = jnp.concatenate([halo_keys, keys], 0).reshape(
        blocks + 1, window, head_local, head_size
    )
    ext_values = jnp.concatenate([halo_values, values], 0).reshape(
        blocks + 1, window, head_local, head_size
    )
    ext_phi = jnp.concatenate([halo_phi, phi_k], 0).reshape(
        blocks + 1, window, head_local, feat_all
    )
    near_keys = jnp.concatenate([ext_keys[:-1], ext_keys[1:]], 1)
    near_values = jnp.concatenate([ext_values[:-1], ext_values[1:]], 1)
    near_phi = jnp.concatenate([ext_phi[:-1], ext_phi[1:]], 1)
    block_q = queries.reshape(blocks, window, head_local, head_size)
    block_phi_q = phi_q.reshape(blocks, window, head_local, feat_all)
    row_pos = lax.broadcasted_iota(jnp.int32, (1, 1, window, 2 * window), 2)
    col_pos = lax.broadcasted_iota(jnp.int32, (1, 1, window, 2 * window), 3)
    block_pos = lax.broadcasted_iota(jnp.int32, (blocks, 1, 1, 2 * window), 0)
    key_live = (block_pos > 0) | (col_pos >= window) | has_prior
    in_window = (col_pos > row_pos) & (col_pos <= row_pos + window) & key_live
    in_far = (col_pos <= row_pos) & key_live
    scores = (
        jnp.einsum("cthd,cshd->chts", block_q, near_keys, preferred_element_type=jnp.float32)
        * score_scale
    )
    top_score = jnp.max(jnp.where(in_window, scores, -jnp.inf), axis=-1)
    damping = jnp.exp(-top_score)
    kernel = jnp.einsum(
        "cthf,cshf->chts", block_phi_q, near_phi, preferred_element_type=jnp.float32
    )
    weights = jnp.where(in_window, jnp.exp(scores - top_score[..., None]), 0.0)
    weights = weights + jnp.where(in_far, damping[..., None] * kernel, 0.0)
    near_num = jnp.einsum(
        "chts,cshd->cthd",
        weights.astype(jnp.bfloat16),
        near_values,
        preferred_element_type=jnp.float32,
    )
    near_den = jnp.swapaxes(jnp.sum(weights, -1), 1, 2)
    span_states = jnp.einsum(
        "cshf,cshd->chfd", ext_phi, ext_values, preferred_element_type=jnp.float32
    )
    span_sums = jnp.sum(ext_phi, axis=1, dtype=jnp.float32)
    send_states = jnp.sum(span_states[:blocks], 0)
    send_sums = jnp.sum(span_sums[:blocks], 0)
    zero_states = jnp.zeros_like(send_states)
    zero_sums = jnp.zeros_like(send_sums)
    prior_states, prior_sums = prefix(
        (send_states, send_sums), "seq", add_pair, (zero_states, zero_sums), False
    )
    lead_states = prior_states[None] + jnp.concatenate(
        [jnp.zeros_like(span_states[:1]), jnp.cumsum(span_states[: blocks - 1], 0)], 0
    )
    lead_sums = prior_sums[None] + jnp.concatenate(
        [jnp.zeros_like(span_sums[:1]), jnp.cumsum(span_sums[: blocks - 1], 0)], 0
    )
    damp_rows = jnp.swapaxes(damping, 1, 2)
    state_num = jnp.einsum(
        "cthf,chfd->cthd",
        block_phi_q,
        lead_states,
        precision=state_precision,
        preferred_element_type=jnp.float32,
    )
    state_den = jnp.einsum(
        "cthf,chf->cth",
        block_phi_q,
        lead_sums,
        precision=state_precision,
        preferred_element_type=jnp.float32,
    )
    numerator = near_num + damp_rows[..., None] * state_num
    denominator = near_den + damp_rows * state_den
    output = numerator / denominator[..., None]
    hybrid = output.astype(jnp.bfloat16).reshape(tok_rows, head_local, head_size)
    block_target = target.reshape(blocks, window, head_local, head_size).astype(jnp.float32)
    d_out = 2.0 * (output - block_target) / total_tokens
    d_numer = d_out / denominator[..., None]
    d_denom = -jnp.sum(d_out * output, -1) / denominator
    d_weight = jnp.einsum(
        "cthd,cshd->chts",
        d_numer.astype(jnp.bfloat16),
        near_values,
        preferred_element_type=jnp.float32,
    )
    d_weight = d_weight + jnp.swapaxes(d_denom, 1, 2)[..., None]
    far_grad = jnp.where(in_far, damping[..., None] * d_weight, 0.0).astype(jnp.bfloat16)
    d_phi_q = jnp.einsum("chts,cshf->cthf", far_grad, near_phi, preferred_element_type=jnp.float32)
    d_phi_q = d_phi_q + damp_rows[..., None] * (
        jnp.einsum("cthd,chfd->cthf", d_numer, lead_states, precision=state_precision)
        + d_denom[..., None] * lead_sums[:, None]
    )
    d_near = jnp.einsum(
        "chts,cthf->cshf", far_grad, block_phi_q, preferred_element_type=jnp.float32
    )
    zero_block = jnp.zeros_like(d_near[:1, :window])
    d_ext = jnp.concatenate([d_near[:, :window], zero_block], 0) + jnp.concatenate(
        [zero_block, d_near[:, window:]], 0
    )
    state_grad = (damp_rows[..., None] * d_numer).astype(jnp.bfloat16)
    grad_states = jnp.einsum(
        "cthf,cthd->chfd", block_phi_q, state_grad, preferred_element_type=jnp.float32
    )
    grad_sums = jnp.einsum(
        "cth,cthf->chf",
        damp_rows * d_denom,
        block_phi_q,
        precision=state_precision,
        preferred_element_type=jnp.float32,
    )
    send_gstates = jnp.sum(grad_states, 0)
    send_gsums = jnp.sum(grad_sums, 0)
    later_states, later_sums = prefix(
        (send_gstates, send_gsums), "seq", add_pair, (zero_states, zero_sums), True
    )
    tail_states = jnp.cumsum(grad_states[::-1], 0)[::-1]
    tail_sums = jnp.cumsum(grad_sums[::-1], 0)[::-1]
    upper_states = jnp.concatenate([tail_states[1:], jnp.zeros_like(span_states[:2])], 0)
    upper_sums = jnp.concatenate([tail_sums[1:], jnp.zeros_like(span_sums[:2])], 0)
    later_stack = jnp.concatenate(
        [
            jnp.broadcast_to(later_states[None], (blocks,) + later_states.shape),
            jnp.zeros_like(span_states[:1]),
        ],
        0,
    )
    later_sum_stack = jnp.concatenate(
        [
            jnp.broadcast_to(later_sums[None], (blocks,) + later_sums.shape),
            jnp.zeros_like(span_sums[:1]),
        ],
        0,
    )
    key_states_grad = upper_states + later_stack
    key_sums_grad = upper_sums + later_sum_stack
    d_ext = d_ext + jnp.einsum(
        "cshd,chfd->cshf",
        ext_values,
        key_states_grad,
        precision=state_precision,
        preferred_element_type=jnp.float32,
    )
    d_ext = d_ext + key_sums_grad[:, None]
    returned = from_behind(d_ext[0], "seq", -1)
    own_grad = d_ext[1:].reshape(tok_rows, head_local, feat_all)
    own_grad = jnp.concatenate([own_grad[:edge_start], own_grad[edge_start:] + returned], 0)
    grad_q = feature_grad(
        queries, q_upper, q_lower, d_phi_q.reshape(tok_rows, head_local, feat_all)
    )
    grad_k = feature_grad(keys, k_upper, k_lower, own_grad)
    summed_q, summed_k = lax.psum((grad_q, grad_k), ("seq", "head"))
    return (hybrid, summed_q, summed_k)


def solution(mesh):
    in_specs = (
        P("seq", "head", None),
        P("seq", "head", None),
        P("seq", "head", None),
        P("seq", "head", None),
        P(),
        P(),
    )
    out_specs = (P("seq", "head", None), P(), P())
    return jax.shard_map(
        per_device, mesh=mesh, in_specs=in_specs, out_specs=out_specs, check_vma=False
    )
```

profile of v0, /device:TPU:1, one launch (start us, length us, event | category | flops | bytes accessed | tf_op | source)
XLA Modules:
  0.0 1034.2 jit_solution(3663511937367038215)
XLA Ops:
  8.3 4.0 collective-permute-start.1
  12.3 1.7 slice.90
  14.0 3.9 collective-permute-start
  25.8 1.7 copy-done.2
  30.8 2.3 fusion.148
  33.1 2.0 concatenate.75
  35.1 2.0 copy.58
  37.1 2.3 fusion.151
  39.5 2.0 concatenate.74
  41.5 2.0 copy.57
  43.5 2.0 copy.63
  45.5 2.0 copy.62
  54.3 2.2 copy.61
  61.8 158.3 %all-gather.1 = f32[1024,128]{1,0:T(8,128)S(1)} all-gather(f32[16,128]{1,0:T(8,128)S(1)} %slice_reduce_fusion.1), channel_id=3, replica_groups=mesh['seq'=64,'head'=2] {'seq'}, dimensions={0}, use_global_device_ids=true | all-gather | bytes 532480 | tf_op jit(solution)/shard_map/all_gather | solution.py:20
  220.1 2.1 fusion.154
  222.2 92.7 %all-gather.7.cloned.1.call-done = f32[1024,128,128]{2,1,0:T(8,128)} async-done(((f32[16,128,128]{2,1,0:T(8,128)}), f32[1024,128,128]{2,1,0:T(8,128)}) %all-gather.7.cloned.1.call-update) | async-done | bytes 67108880 | tf_op jit(solution)/shard_map/all_gather | solution.py:20
  314.9 104.6 %while.34 = (s32[]{:T(128)}, f32[16,128,128]{2,1,0:T(8,128)S(1)}, f32[16,128]{1,0:T(8,128)S(1)}, s32[]{:T(128)}, f32[64,16,128,128]{3,2,1,0:T(8,128)}, /*index=5*/f32[64,16,128]{2,1,0:T(8,128)S(1)}, s32[]{:T(128)}, s32[]{:T(128)}) while((s32[]{:T(128)}, f32[16,128,128]{2,1,0:T(8,128)S(1)}, f32[16,128]{1,0:T(8,128)S(1)}, ...), condition=%wide.region_17.18_spmd.clone, body=%wide.region_16.17_spmd.clone.sunk | while | flops 792580 | bytes 3170427 | solution.py:33
  314.9 1.6 add_select_fusion.8
  318.2 1.6 add_select_fusion.8
  321.5 1.6 add_select_fusion.8
  324.7 1.6 add_select_fusion.8
  328.0 1.6 add_select_fusion.8
  331.3 1.6 add_select_fusion.8
  334.5 1.6 add_select_fusion.8
  336.2 1.6 add_select_fusion.8
  337.8 1.6 add_select_fusion.8
  339.4 1.6 add_select_fusion.8
  341.1 1.6 add_select_fusion.8
  342.7 1.6 add_select_fusion.8
  344.3 1.6 add_select_fusion.8
  346.0 1.6 add_select_fusion.8
  349.2 1.6 add_select_fusion.8
  352.5 1.6 add_select_fusion.8
  355.8 1.6 add_select_fusion.8
  359.0 1.6 add_select_fusion.8
  362.3 1.6 add_select_fusion.8
  365.6 1.6 add_select_fusion.8
  367.2 1.6 add_select_fusion.8
  368.8 1.6 add_select_fusion.8
  370.5 1.6 add_select_fusion.8
  372.1 1.6 add_select_fusion.8
  373.7 1.6 add_select_fusion.8
  375.4 1.6 add_select_fusion.8
  377.0 1.6 add_select_fusion.8
  380.3 1.6 add_select_fusion.8
  421.2 1.7 fusion.72
  422.9 3.2 fusion.155
  426.3 2.5 fusion.34
  430.9 2.4 fusion.30
  434.7 3.4 rev.8
  438.1 1.8 fusion.188
  441.0 163.2 %all-gather.3 = f32[1024,128]{1,0:T(8,128)} all-gather(f32[16,128]{1,0:T(8,128)S(1)} %reduce_sum.167), channel_id=5, replica_groups=mesh['seq'=64,'head'=2] {'seq'}, dimensions={0}, use_global_device_ids=true | all-gather | bytes 532480 | tf_op jit(solution)/shard_map/all_gather | solution.py:20
  604.7 2.8 fusion.146
  607.4 99.0 %all-gather.9.cloned.1.call-done = f32[1024,128,128]{2,1,0:T(8,128)} async-done(((f32[16,128,128]{2,1,0:T(8,128)}), f32[1024,128,128]{2,1,0:T(8,128)}) %all-gather.9.cloned.1.call-update) | async-done | bytes 67108880 | tf_op jit(solution)/shard_map/all_gather | solution.py:20
  706.4 147.0 %while.35 = (s32[]{:T(128)}, f32[16,128,128]{2,1,0:T(8,128)S(1)}, f32[16,128]{1,0:T(8,128)S(1)}, s32[]{:T(128)}, f32[64,16,128,128]{3,2,1,0:T(8,128)}, /*index=5...) while((s32[]{:T(128)}, f32[16,128,128]{2,1,0:T(8,128)S(1)}, ...), condition=%wide.region_27.28_spmd.clone, body=%wide.region_26.27_spmd.clone.sunk | while | flops 792584 | bytes 3170489 | solution.py:33
  706.4 1.6 add_select_fusion.10
  855.2 3.1 fusion.12
  864.0 1.7 copy.87
  867.3 2.6 fusion.63
  870.0 6.2 collective-permute-done.2
  878.9 1.6 fusion.58
  880.5 2.4 fusion.64
  882.9 2.2 copy.68
  885.1 139.8 %all-reduce.11.cloned.1.call-done = (f32[128,64]{0,1:T(8,128)}, f32[128,64]{0,1:T(8,128)}) async-done(((f32[128,64]{0,1:T(8,128)}, f32[128,64]{0,1:T(8,128)}), (f32[128,64]{0,1:T(8,128)}, f32[128,64]{0,1:T(8,128)})) %all-reduce.11.cloned.1.call-update) | async-done | bytes 65552 | tf_op jit(solution)/shard_map/psum | solution.py:229
  (383 shorter events, 248.4 us)
Async XLA Ops:
  7.2 23.6 %copy-start = (bf16[128,64]{0,1:T(8,128)(2,1)S(1)}, bf16[128,64]{0,1:T(8,128)(2,1)}, u32[]{:S(2)}) copy-start(bf16[128,64]{0,1:T(8,128)(2,1)} %param.14) | copy-start | bytes 49156
  7.2 12.1 %copy-start.12 = (bf16[128,16,128]{2,1,0:T(8,128)(2,1)S(1)}, bf16[128,16,128]{2,1,0:T(8,128)(2,1)}, u32[]{:S(2)}) copy-start(bf16[128,16,128]{2,1,0:T(8,128)(2,1)} %param.11) | copy-start | bytes 1572868
  7.2 12.1 %copy-start.37 = (bf16[128,64]{0,1:T(8,128)(2,1)S(1)}, bf16[128,64]{0,1:T(8,128)(2,1)}, u32[]{:S(2)}) copy-start(bf16[128,64]{0,1:T(8,128)(2,1)} %param.15) | copy-start | bytes 49156
  7.2 307.7 %all-gather.7.cloned.1.call-start = ((), (), s32[]{:S(2)}) async-start(), calls=%async_computation | async-start | bytes 68157440 | tf_op jit(solution)/shard_map/all_gather | solution.py:20
  8.3 11.6 %collective-permute-start.1 = (bf16[64,16,128]{2,1,0:T(8,128)(2,1)S(1)}, bf16[64,16,128]{2,1,0:T(8,128)(2,1)S(1)}, u32[]{:S(2)}, u32[]{:S(2)}) collective-permute-start(bf16[64,16,128]{2,1,0:T(8,128)(2,1)S(1)} %slice.94), channel_id=1, source_target_pairs={{0,2},{2,4},{4,6},{6,8},{8,10},{10,12},{12,14},{14,16},{16,18},{18... | collective-permute-start | bytes 786440 | tf_op jit(solution)/shard_map/ppermute | solution.py:15
  14.0 9.2 collective-permute-start
  19.3 1.1 copy-start.29
  19.7 1.2 copy-start.20
  19.8 1.1 copy-start.33
  21.4 2.8 copy-start.16
  24.3 0.9 copy-start.9
  25.8 1.7 copy-start.2
  28.6 677.8 %all-gather.9.cloned.1.call-start = ((), (), s32[]{:S(2)}) async-start(), calls=%async_computation.1 | async-start | bytes 68157440 | tf_op jit(solution)/shard_map/all_gather | solution.py:20
  47.5 2.7 copy-start.30
  50.0 372.9 %copy-start.6 = (bf16[2,64,16,128]{3,1,2,0:T(8,128)(2,1)}, bf16[2,64,16,128]{3,1,2,0:T(8,128)(2,1)S(1)}, u32[]{:S(2)}) copy-start(bf16[2,64,16,128]{3,1,2,0:T(8,128)(2,1)S(1)} %pad_maximum_fusion.2) | copy-start | bytes 1572868
  50.2 3.3 copy-start.10
  56.6 2.9 copy-start.32
  56.6 2.9 copy-start.36
  57.9 162.3 %copy-start.26 = (bf16[2,64,16,128]{3,1,2,0:T(8,128)(2,1)}, bf16[2,64,16,128]{3,1,2,0:T(8,128)(2,1)S(1)}, u32[]{:S(2)}) copy-start(bf16[2,64,16,128]{3,1,2,0:T(8,128)(2,1)S(1)} %copy.64) | copy-start | bytes 1572868
  59.3 1.1 copy-start.21
  59.4 1.2 copy-start.34
  59.5 1.1 copy-start.17
  60.4 159.7 %copy-start.22 = (bf16[2,64,16,64]{3,1,2,0:T(8,128)(2,1)S(1)}, bf16[2,64,16,64]{3,1,2,0:T(8,128)(2,1)}, u32[]{:S(2)}) copy-start(bf16[2,64,16,64]{3,1,2,0:T(8,128)(2,1)} %copy.63) | copy-start | bytes 786436
  60.4 159.7 %copy-start.24 = (bf16[2,64,16,64]{3,1,2,0:T(8,128)(2,1)S(1)}, bf16[2,64,16,64]{3,1,2,0:T(8,128)(2,1)}, u32[]{:S(2)}) copy-start(bf16[2,64,16,64]{3,1,2,0:T(8,128)(2,1)} %copy.62) | copy-start | bytes 786436
  60.8 1.0 copy-start.18
  314.9 104.6 %slice-start = ((f32[3,16,128]{2,1,0:T(8,128)}), f32[1,16,128]{2,1,0:T(8,128)S(1)}, s32[]{:S(2)}) async-start(f32[3,16,128]{2,1,0:T(8,128)} %copy-done.34), calls=%async_computation.3 | async-start | bytes 16384 | tf_op jit(solution)/shard_map/slice | solution.py:133
  419.5 1.5 copy-start.19
  419.5 1.5 copy-start.28
  419.5 1.7 copy-start.38
  422.9 3.2 copy-start.4
  426.2 598.7 %all-reduce.11.cloned.1.call-start = ((), (), s32[]{:S(2)}) async-start(), calls=%async_computation.2 | async-start | bytes 131072 | tf_op jit(solution)/shard_map/psum | solution.py:229
  426.2 3.4 copy-start.23
  426.2 3.4 copy-start.25
  426.3 3.4 copy-start.27
  428.8 0.8 copy-start.14
  429.6 1.2 copy-start.5
  433.2 1.0 copy-start.7
  439.9 164.3 %copy-start.15 = (bf16[2,16,64,128]{3,2,1,0:T(8,128)(2,1)S(1)}, bf16[2,16,64,128]{3,2,1,0:T(8,128)(2,1)}, u32[]{:S(2)}) copy-start(bf16[2,16,64,128]{3,2,1,0:T(8,128)(2,1)} %copy-done.14) | copy-start | bytes 1572868
  441.0 166.4 %copy-start.35 = (f32[2,16,128]{2,1,0:T(8,128)}, f32[2,16,128]{2,1,0:T(8,128)S(1)}, u32[]{:S(2)}) copy-start(f32[2,16,128]{2,1,0:T(8,128)S(1)} %fusion.189) | copy-start | bytes 49156
  706.4 147.0 %slice-start.1 = ((f32[2,16,128]{2,1,0:T(8,128)}), f32[1,16,128]{2,1,0:T(8,128)S(1)}, s32[]{:S(2)}) async-start(f32[2,16,128]{2,1,0:T(8,128)} %copy-done.35), calls=%async_computation.4 | async-start | bytes 16384 | tf_op jit(solution)/shard_map/slice | solution.py:197
  853.4 1.6 copy-start.8
  853.5 1.8 copy-start.11
  858.3 1.7 copy-start.3
  861.1 15.0 %collective-permute-start.2 = (f32[64,16,128]{2,1,0:T(8,128)}, f32[64,16,128]{2,1,0:T(8,128)}, u32[]{:S(2)}, u32[]{:S(2)}) collective-permute-start(f32[64,16,128]{2,1,0:T(8,128)} %copy.77), channel_id=1, source_target_pairs={{2,0},{4,2},{6,4},{8,6},{10,8},{12,10},{14,12},{16,14},{18,16},{20... | collective-permute-start | bytes 1572872 | tf_op jit(solution)/shard_map/ppermute | solution.py:15
  864.0 2.9 copy-start.31
  878.9 1.6 copy-start.13
  878.9 148.7 %copy-start.1 = (bf16[128,64]{0,1:T(8,128)(2,1)S(1)}, bf16[128,64]{0,1:T(8,128)(2,1)}, u32[]{:S(2)}) copy-start(bf16[128,64]{0,1:T(8,128)(2,1)} %param.14) | copy-start | bytes 49156
Sparse Core Ops, SparseCore 0:
  28.7 286.1 all-gather.6
  426.3 280.0 all-gather.8
  883.0 141.7 all-reduce.10
where the time goes:
time: 1040 us; the launch traced here: 1030 us
  waiting for transfers between devices  338 us (32%)
  blocking collectives  322 us (31%)
  other arithmetic  261 us (25%)
  local copies, waits for them, and re-layouts  55.8 us (5%)
  matrix products  31.6 us (3%)
  between operations  14.5 us (1%)
    all_gather x2, blocking collectives, prefix(): everything = jax.tree.map(lambda part: lax.all_gather(part, axis), array)  322 us
    select_n x256, other arithmetic, turn(): return jax.tree.map(lambda a, b: jnp.where(reached, a, b), new, before)  249 us
    all_gather x2, waiting for transfers between devices, prefix(): everything = jax.tree.map(lambda part: lax.all_gather(part, axis), array)  192 us
    psum x1, waiting for transfers between devices, per_device(): summed_q, summed_k = lax.psum((grad_q, grad_k), ('seq', 'head'))  140 us
  transfers between devices with their start and end apart: 6, of which 5 were waited for; matrix products, arithmetic and copies ran while one was open for 6% of the time, Pallas kernels for 0%

commit v1 on v0

v1 whole, which is shorter than its diff:
```python
import functools

import jax
import jax.numpy as jnp
from jax import lax
from jax.experimental import pallas as pl
from jax.experimental.pallas import tpu as pltpu
from jax.sharding import PartitionSpec as P

WINDOW = 64
FEAT = 64
PLANE = 16
ROWS = 136
MESH = pl.DeviceIdType.MESH
F32 = jnp.float32
BF16 = jnp.bfloat16
VMEM_LIMIT = 56 * 1024 * 1024


def dot_nn(a, b):
    return lax.dot_general(a, b, (((1,), (0,)), ((), ())), preferred_element_type=F32)


def dot_nt(a, b):
    return lax.dot_general(a, b, (((1,), (1,)), ((), ())), preferred_element_type=F32)


def dot_tn(a, b):
    return lax.dot_general(a, b, (((0,), (0,)), ((), ())), preferred_element_type=F32)


def split(x):
    high = x.astype(BF16)
    return high, (x - high.astype(F32)).astype(BF16)


def left_half(shape):
    return lax.broadcasted_iota(jnp.int32, shape, len(shape) - 1) < FEAT


def features(x, pair_map):
    hidden = dot_nn(x, pair_map)
    left = left_half(hidden.shape)
    top_left = jnp.max(jnp.where(left, hidden, -jnp.inf), -1, keepdims=True)
    top_right = jnp.max(jnp.where(left, -jnp.inf, hidden), -1, keepdims=True)
    e = jnp.exp(hidden - jnp.where(left, top_left, top_right))
    sum_left = jnp.sum(jnp.where(left, e, 0.0), -1, keepdims=True)
    sum_right = jnp.sum(jnp.where(left, 0.0, e), -1, keepdims=True)
    return e * jnp.where(left, 1.0 / sum_left, 1.0 / sum_right)


def feature_grad(x, soft, upstream):
    left = left_half(soft.shape)
    product = soft * upstream
    inner_left = jnp.sum(jnp.where(left, product, 0.0), -1, keepdims=True)
    inner_right = jnp.sum(jnp.where(left, 0.0, product), -1, keepdims=True)
    part = soft * (upstream - jnp.where(left, inner_left, inner_right))
    u = part - pltpu.roll(part, FEAT, 1)
    return dot_tn(x, u.astype(BF16))


def head_rows(ref, head, rows, heads):
    return ref[pl.ds(head, rows, stride=heads), :]


def widen(src, dst):
    dst[...] = src[...].astype(F32)


def key_kernel(heads, k_ref, v_ref, map_ref, state_ref, soft_ref, kh_ref, vh_ref, k_wide, v_wide):
    rows = k_ref.shape[0] // heads
    widen(k_ref, k_wide)
    widen(v_ref, v_wide)
    pair_map = map_ref[...]

    def step(head, carry):
        k = head_rows(k_wide, head, rows, heads).astype(BF16)
        v = head_rows(v_wide, head, rows, heads).astype(BF16)
        kh_ref[head] = k
        vh_ref[head] = v
        soft = features(k, pair_map)
        soft_ref[head] = soft
        phi = soft.astype(BF16)
        state_ref[head, :128, :] = dot_tn(phi, v)
        state_ref[head, 128:, :] = jnp.broadcast_to(
            jnp.sum(phi.astype(F32), 0, keepdims=True), (ROWS - 128, 128)
        )
        return carry

    lax.fori_loop(0, heads, step, 0)


def main_kernel(
    heads, total_tokens, q_ref, t_ref, k_ref, v_ref, softk_ref, hk_ref, hv_ref, p_ref, mq_ref, mk_ref,
    out_ref, g_ref, gq_ref, near_ref, back_ref, q_wide, t_wide, hk_wide, hv_wide, out_wide,
):
    rows = q_ref.shape[0] // heads
    w = WINDOW
    has_prior = lax.axis_index("seq") > 0
    widen(q_ref, q_wide)
    widen(t_ref, t_wide)
    widen(hk_ref, hk_wide)
    widen(hv_ref, hv_wide)
    map_q = mq_ref[...]
    map_k = mk_ref[...]
    gq_ref[...] = jnp.zeros_like(gq_ref)
    row = lax.broadcasted_iota(jnp.int32, (w, 2 * w), 0)
    col = lax.broadcasted_iota(jnp.int32, (w, 2 * w), 1)
    scale = 128 ** (-0.5)

    def step(head, carry):
        q = head_rows(q_wide, head, rows, heads).astype(BF16)
        target = head_rows(t_wide, head, rows, heads)
        k, v = k_ref[head], v_ref[head]
        hk = head_rows(hk_wide, head, w, heads).astype(BF16)
        hv = head_rows(hv_wide, head, w, heads).astype(BF16)
        soft_q = features(q, map_q)
        phi_q = soft_q.astype(BF16)
        phi_k = softk_ref[head].astype(BF16)
        phi_h = jnp.where(has_prior, features(hk, map_k), 0.0).astype(BF16)
        state1 = p_ref[head, :128, :]
        sum1 = p_ref[head, 128:129, :]
        state0 = state1 - dot_tn(phi_h, hv)
        sum0 = sum1 - jnp.sum(phi_h.astype(F32), 0, keepdims=True)
        d_phi, near, gstate, gsum = [], [], [], []
        for c in range(2):
            if c == 0:
                kn = jnp.concatenate([hk, k[:w]], 0)
                vn = jnp.concatenate([hv, v[:w]], 0)
                pn = jnp.concatenate([phi_h, phi_k[:w]], 0)
                state, ksum = state0, sum0
                live = (col >= w) | has_prior
                in_window = (col > row) & (col <= row + w) & live
                in_far = (col <= row) & live
            else:
                kn, vn, pn = k, v, phi_k
                state, ksum = state1, sum1
                in_window = (col > row) & (col <= row + w)
                in_far = col <= row
            qb = q[c * w : (c + 1) * w]
            pq = phi_q[c * w : (c + 1) * w]
            tb = target[c * w : (c + 1) * w]
            scores = jnp.where(in_window, dot_nt(qb, kn) * scale, -jnp.inf)
            top = jnp.max(scores, -1, keepdims=True)
            damping = jnp.exp(-top)
            weight = jnp.exp(scores - top) + jnp.where(in_far, damping * dot_nt(pq, pn), 0.0)
            state_high, state_low = split(state)
            state_num = dot_nn(pq, state_high) + dot_nn(pq, state_low)
            state_den = jnp.sum(pq.astype(F32) * ksum, -1, keepdims=True)
            numer = dot_nn(weight.astype(BF16), vn) + damping * state_num
            denom = jnp.sum(weight, -1, keepdims=True) + damping * state_den
            inverse = 1.0 / denom
            output = numer * inverse
            out_wide[pl.ds(c * w * heads + head, w, stride=heads), :] = output
            d_out = (output - tb) * (2.0 / total_tokens)
            d_numer = d_out * inverse
            d_denom = -jnp.sum(d_out * output, -1, keepdims=True) * inverse
            dn_high, dn_low = split(d_numer)
            d_weight = dot_nt(dn_high, vn) + d_denom
            far_grad = jnp.where(in_far, damping * d_weight, 0.0).astype(BF16)
            through = dot_nt(dn_high, state_high) + dot_nt(dn_high, state_low) + dot_nt(dn_low, state_high)
            d_phi.append(dot_nn(far_grad, pn) + damping * (through + d_denom * ksum))
            near.append(dot_tn(far_grad, pq))
            grad = (damping * d_numer).astype(BF16)
            gstate.append(dot_tn(pq, grad))
            gsum.append(jnp.sum(damping * d_denom * pq.astype(F32), 0, keepdims=True))
        gq_ref[...] += feature_grad(q, soft_q, jnp.concatenate(d_phi, 0))
        g_ref[head, :128, :] = gstate[0] + gstate[1]
        g_ref[head, 128:, :] = jnp.broadcast_to(gsum[0] + gsum[1], (ROWS - 128, 128))
        near_ref[head, :w, :] = near[0][w:] + near[1][:w]
        near_ref[head, w:, :] = near[1][w:]
        first_high, first_low = split(gstate[0])
        back_ref[head] = near[0][:w] - (dot_nt(hv, first_high) + dot_nt(hv, first_low) + gsum[0])
        return carry

    lax.fori_loop(0, heads, step, 0)
    out_ref[...] = out_wide[...].astype(BF16)


def last_kernel(heads, later_ref, near_ref, back_ref, k_ref, v_ref, softk_ref, gq_ref, out_ref):
    w = WINDOW
    out_ref[...] = jnp.zeros_like(out_ref)

    def step(head, carry):
        v, k = v_ref[head], k_ref[head]
        high, low = split(later_ref[head, :128, :])
        near = near_ref[head]
        near = jnp.concatenate([near[:w], near[w:] + back_ref[head]], 0)
        d_phi = near + dot_nt(v, high) + dot_nt(v, low) + later_ref[head, 128:129, :]
        out_ref[...] += feature_grad(k, softk_ref[head], d_phi)
        return carry

    lax.fori_loop(0, heads, step, 0)
    out_ref[...] = jnp.where(left_half(out_ref.shape), gq_ref[...], -out_ref[...])


def scan_kernel(reverse, x_ref, out_ref, parts, ztotals, send1, recv1, sendz, recvz, send2, recv2):
    me = lax.axis_index("seq")
    layers = lax.axis_size("seq") // PLANE
    z, p = me // PLANE, me % PLANE

    barrier = pltpu.get_barrier_semaphore()

    def greet(i, carry):
        pl.semaphore_signal(
            barrier, inc=1, device_id={"seq": z * PLANE + (p + i) % PLANE}, device_id_type=MESH
        )
        return carry

    lax.fori_loop(1, PLANE, greet, 0)
    for i in range(1, layers):
        pl.semaphore_signal(
            barrier, inc=1, device_id={"seq": ((z + i) % layers) * PLANE + p}, device_id_type=MESH
        )
    pl.semaphore_wait(barrier, PLANE - 1 + layers - 1)

    def up(i):
        to = (p + i) % PLANE
        return pltpu.make_async_remote_copy(
            src_ref=x_ref.at[to], dst_ref=parts.at[p], send_sem=send1.at[to], recv_sem=recv1.at[p],
            device_id={"seq": z * PLANE + to}, device_id_type=MESH,
        )

    def up_from(k):
        return pltpu.make_async_remote_copy(
            src_ref=x_ref.at[k], dst_ref=parts.at[k], send_sem=send1.at[k], recv_sem=recv1.at[k],
            device_id={"seq": z * PLANE + k}, device_id_type=MESH,
        )

    def start_up(i, carry):
        up(i).start()
        return carry

    lax.fori_loop(1, PLANE, start_up, 0)
    parts[p] = x_ref[p]

    def gather(i, total):
        k = PLANE - 1 - i if reverse else i

        @pl.when(k != p)
        def _():
            up_from(k).wait_recv()

        part = parts[k]
        parts[k] = total
        return total + part

    total = lax.fori_loop(0, PLANE, gather, jnp.zeros(x_ref.shape[1:], F32))
    ztotals[z] = total

    def across(i, to):
        other = (z + i) % layers
        return pltpu.make_async_remote_copy(
            src_ref=ztotals.at[z], dst_ref=ztotals.at[z if to else other],
            send_sem=sendz.at[other], recv_sem=recvz.at[z if to else other],
            device_id={"seq": other * PLANE + p}, device_id_type=MESH,
        )

    for i in range(1, layers):
        across(i, True).start()
    for i in range(1, layers):
        across(i, False).wait_recv()
    base = jnp.zeros(x_ref.shape[1:], F32)
    for k in range(layers):
        reached = k > z if reverse else k < z
        base = base + jnp.where(reached, ztotals[k], 0.0)

    def down(k, into):
        return pltpu.make_async_remote_copy(
            src_ref=parts.at[k], dst_ref=out_ref.at[into], send_sem=send2.at[k], recv_sem=recv2.at[into],
            device_id={"seq": z * PLANE + k}, device_id_type=MESH,
        )

    def start_down(i, carry):
        to = (p + i) % PLANE
        parts[to] = parts[to] + base
        down(to, p).start()
        return carry

    lax.fori_loop(1, PLANE, start_down, 0)
    out_ref[p] = parts[p] + base

    def finish(i, carry):
        k = (p + i) % PLANE
        down(k, k).wait_recv()
        down(k, k).wait_send()
        up_from(k).wait_send()
        return carry

    lax.fori_loop(1, PLANE, finish, 0)
    for i in range(1, layers):
        across(i, True).wait_send()


def sum_kernel(x_ref, out_ref, parts, totals, send1, recv1, sendz, recvz, send2, recv2):
    me, core = lax.axis_index("seq"), lax.axis_index("head")
    layers = lax.axis_size("seq") // PLANE
    cores = lax.axis_size("head")
    others = layers * cores
    z, p = me // PLANE, me % PLANE
    here = z * cores + core
    rows = x_ref.shape[0] // PLANE

    def rows_of(k):
        return pl.ds(pl.multiple_of(k * rows, rows), rows)

    def beyond(i):
        at = (here + i) % others
        return at, {"seq": (at // cores) * PLANE + p, "head": at % cores}

    barrier = pltpu.get_barrier_semaphore()

    def greet(i, carry):
        pl.semaphore_signal(
            barrier, inc=1, device_id={"seq": z * PLANE + (p + i) % PLANE}, device_id_type=MESH
        )
        return carry

    lax.fori_loop(1, PLANE, greet, 0)

    def greet_beyond(i, carry):
        pl.semaphore_signal(barrier, inc=1, device_id=beyond(i)[1], device_id_type=MESH)
        return carry

    lax.fori_loop(1, others, greet_beyond, 0)
    pl.semaphore_wait(barrier, PLANE - 1 + others - 1)

    def up(k, into):
        return pltpu.make_async_remote_copy(
            src_ref=x_ref.at[rows_of(k)], dst_ref=parts.at[into], send_sem=send1.at[k], recv_sem=recv1.at[into],
            device_id={"seq": z * PLANE + k}, device_id_type=MESH,
        )

    def start_up(i, carry):
        up((p + i) % PLANE, p).start()
        return carry

    lax.fori_loop(1, PLANE, start_up, 0)
    parts[p] = x_ref[rows_of(p)]

    def gather(k, total):
        @pl.when(k != p)
        def _():
            up(k, k).wait_recv()

        return total + parts[k]

    zero = jnp.zeros((rows, x_ref.shape[1]), F32)
    totals[here] = lax.fori_loop(0, PLANE, gather, zero)

    def across(i, to):
        at, device = beyond(i)
        into = here if to else at
        return pltpu.make_async_remote_copy(
            src_ref=totals.at[here], dst_ref=totals.at[into], send_sem=sendz.at[at], recv_sem=recvz.at[into],
            device_id=device, device_id_type=MESH,
        )

    def start_across(i, carry):
        across(i, True).start()
        return carry

    def await_across(i, carry):
        across(i, False).wait_recv()
        across(i, False).wait_send()
        return carry

    lax.fori_loop(1, others, start_across, 0)
    lax.fori_loop(1, others, await_across, 0)
    result = zero
    for k in range(others):
        result = result + totals[k]
    out_ref[rows_of(p)] = result

    def down(k, into):
        return pltpu.make_async_remote_copy(
            src_ref=out_ref.at[rows_of(p)], dst_ref=out_ref.at[rows_of(into)],
            send_sem=send2.at[k], recv_sem=recv2.at[into],
            device_id={"seq": z * PLANE + k}, device_id_type=MESH,
        )

    def start_down(i, carry):
        down((p + i) % PLANE, p).start()
        return carry

    lax.fori_loop(1, PLANE, start_down, 0)

    def finish(i, carry):
        k = (p + i) % PLANE
        down(k, k).wait_recv()
        down(k, k).wait_send()
        up(k, k).wait_send()
        return carry

    lax.fori_loop(1, PLANE, finish, 0)


def in_vmem(count):
    return [pl.BlockSpec(memory_space=pltpu.VMEM)] * count


def call(kernel, outs, scratch, args, **params):
    shapes = [jax.ShapeDtypeStruct(shape, dtype) for shape, dtype in outs]
    return pl.pallas_call(
        kernel,
        out_shape=shapes,
        in_specs=in_vmem(len(args)),
        out_specs=in_vmem(len(outs)),
        scratch_shapes=scratch,
        compiler_params=pltpu.CompilerParams(vmem_limit_bytes=VMEM_LIMIT, **params),
    )(*args)


def scan(x, reverse, collective_id):
    layers = lax.axis_size("seq") // PLANE
    dma = pltpu.SemaphoreType.DMA
    return call(
        functools.partial(scan_kernel, reverse),
        [(x.shape, F32)],
        [
            pltpu.VMEM(x.shape, F32),
            pltpu.VMEM((layers,) + x.shape[1:], F32),
            dma((PLANE,)), dma((PLANE,)), dma((layers,)), dma((layers,)), dma((PLANE,)), dma((PLANE,)),
        ],
        (x,),
        collective_id=collective_id,
        has_side_effects=True,
    )[0]


def sum_all(x, collective_id):
    others = lax.axis_size("seq") // PLANE * lax.axis_size("head")
    part = (x.shape[0] // PLANE, x.shape[1])
    dma = pltpu.SemaphoreType.DMA
    return call(
        sum_kernel,
        [(x.shape, F32)],
        [
            pltpu.VMEM((PLANE,) + part, F32),
            pltpu.VMEM((others,) + part, F32),
            dma((PLANE,)), dma((PLANE,)), dma((others,)), dma((others,)), dma((PLANE,)), dma((PLANE,)),
        ],
        (x,),
        collective_id=collective_id,
        has_side_effects=True,
    )[0]


def shifted(value, steps):
    count = lax.axis_size("seq")
    first, last = max(0, -steps), min(count, count - steps)
    return lax.ppermute(value, "seq", [(source, source + steps) for source in range(first, last)])


def per_device(queries, keys, values, target, map_q, map_k):
    rows, heads, size = queries.shape
    total_tokens = rows * lax.axis_size("seq")
    flat = (rows * heads, size)
    halo = (WINDOW * heads, size)
    pair_q = jnp.concatenate([map_q, -map_q], 1)
    pair_k = jnp.concatenate([map_k, -map_k], 1)
    edge = rows - WINDOW
    halo_keys, halo_values = shifted((keys[edge:], values[edge:]), 1)
    state, soft_k, k_heads, v_heads = call(
        functools.partial(key_kernel, heads),
        [
            ((heads, ROWS, size), F32),
            ((heads, rows, size), F32),
            ((heads, rows, size), BF16),
            ((heads, rows, size), BF16),
        ],
        [pltpu.VMEM(flat, F32), pltpu.VMEM(flat, F32)],
        (keys.reshape(flat), values.reshape(flat), pair_k),
    )
    prior = scan(state, False, 0)
    hybrid, gstate, grad_q, near, back = call(
        functools.partial(main_kernel, heads, total_tokens),
        [
            (flat, BF16),
            ((heads, ROWS, size), F32),
            ((size, size), F32),
            ((heads, rows, size), F32),
            ((heads, WINDOW, size), F32),
        ],
        [pltpu.VMEM(flat, F32), pltpu.VMEM(flat, F32), pltpu.VMEM(halo, F32), pltpu.VMEM(halo, F32), pltpu.VMEM(flat, F32)],
        (
            queries.reshape(flat), target.reshape(flat), k_heads, v_heads, soft_k,
            halo_keys.reshape(halo), halo_values.reshape(halo), prior, pair_q, pair_k,
        ),
    )
    returned = shifted(back, -1)
    later = scan(gstate, True, 1)
    (packed,) = call(
        functools.partial(last_kernel, heads),
        [((size, size), F32)],
        [],
        (later, near, returned, k_heads, v_heads, soft_k, grad_q),
    )
    summed = sum_all(packed, 2)
    return hybrid.reshape(rows, heads, size), summed[:, :FEAT], summed[:, FEAT:]


def solution(mesh):
    tokens = P("seq", "head", None)
    return jax.shard_map(
        per_device,
        mesh=mesh,
        in_specs=(tokens, tokens, tokens, tokens, P(), P()),
        out_specs=(tokens, P(), P()),
        check_vma=False,
    )
```

time: 1040 us -> 189 us (0.18)
  waiting for transfers between devices: 338 us -> 0.01 us
  blocking collectives: 322 us -> 0 us
  other arithmetic: 261 us -> 1.47 us
  Pallas kernels: 0 us -> 171 us
  local copies, waits for them, and re-layouts: 55.8 us -> 7.14 us
  matrix products: 31.6 us -> 0 us
  between operations: 14.5 us -> 0.78 us
    all_gather x2 -> x0, blocking collectives: 322 us -> none  [prefix(): everything = jax.tree.map(lambda part: lax.all_gather(part, axis), array)]
    select_n x257 -> x0, other arithmetic: 249 us -> none  [the longest x256 249 us: turn(): return jax.tree.map(lambda a, b: jnp.where(reached, a, b), new, before)]
    all_gather x2 -> x0, waiting for transfers between devices: 192 us -> none  [prefix(): everything = jax.tree.map(lambda part: lax.all_gather(part, axis), array)]
    pallas_call x0 -> x6, Pallas kernels: none -> 171 us  [call(): pl.pallas_call(kernel, out_shape=shapes, in_specs=in_vmem(len(args)), out...]
    psum x1 -> x0, waiting for transfers between devices: 140 us -> none  [per_device(): summed_q, summed_k = lax.psum((grad_q, grad_k), ('seq', 'head'))]
    dot_general x15 -> x0, matrix products: 24.2 us -> none  [the longest x2 5 us: feature_grad(): jnp.einsum('thd,thf->df', inputs, inner_grad.astype(jnp.bfloat16), prefer...]
    concatenate x11 -> x0, local copies, waits for them, and re-layouts: 15.2 us -> none  [the longest x8 14.2 us: feature_map(): jnp.concatenate([upper_soft, lower_soft], -1).astype(jnp.bfloat16)]
    slice x17 -> x3, local copies, waits for them, and re-layouts: 15.8 us -> 2.94 us  [the longest x2 1.94 us: per_device(): halo_keys, halo_values = shifted((keys[edge:], values[edge:]), 1)]
  transfers between devices with their start and end apart: 6 -> 3, of which waited for: 5 -> 0; matrix products, arithmetic and copies ran while one was open for 6% -> 2% of each run, Pallas kernels for 0% -> 54%
where the time goes in v1:
time: 189 us
  Pallas kernels  171 us (90%)
  starting transfers between devices  8.53 us (5%)
  local copies, waits for them, and re-layouts  7.14 us (4%)
    pallas_call x6, Pallas kernels, call(): pl.pallas_call(kernel, out_shape=shapes, in_specs=in_vmem(len(args)), out...  171 us
    ppermute x3, starting transfers between devices, shifted(): lax.ppermute(value, 'seq', [(source, source + steps) for source in range(...  8.53 us
    unnamed x12, local copies, waits for them, and re-layouts  3.96 us
  transfers between devices with their start and end apart: 3, of which 0 were waited for; matrix products, arithmetic and copies ran while one was open for 2% of the time, Pallas kernels for 54%

profile of v1, /device:TPU:1, one launch (start us, length us, event | category | flops | bytes accessed | tf_op | source)
XLA Modules:
  0.0 188.6 jit_solution(3691283033052800233)
XLA Ops:
  0.6 0.0 copy-start.3
  0.6 1.0 slice.13
  1.6 4.0 %collective-permute-start.1 = (bf16[64,16,128]{2,1,0:T(8,128)(2,1)S(1)}, bf16[64,16,128]{2,1,0:T(8,128)(2,1)S(1)}, u32[]{:S(2)}, u32[]{:S(2)}) collective-permute-start(bf16[64,16,128]{2,1,0:T(8,128)(2,1)S(1)} %slice.13), channel_id=1, source_target_pairs={{0,2},{2,4},{4,6},{6,8},{8,10},{10,12},{12,14},{14,16},{16,18},{18... | collective-permute-start | bytes 786440 | tf_op jit(solution)/shard_map/ppermute | solution.py:452
  5.7 1.0 slice.12
  6.6 3.2 %collective-permute-start = (bf16[64,16,128]{2,1,0:T(8,128)(2,1)S(1)}, bf16[64,16,128]{2,1,0:T(8,128)(2,1)S(1)}, u32[]{:S(2)}, u32[]{:S(2)}) collective-permute-start(bf16[64,16,128]{2,1,0:T(8,128)(2,1)S(1)} %slice.12), channel_id=1, source_target_pairs={{0,2},{2,4},{4,6},{6,8},{8,10},{10,12},{12,14},{14,16},{16,18},{18... | collective-permute-start | bytes 786440 | tf_op jit(solution)/shard_map/ppermute | solution.py:452
  9.9 0.7 neg.7
  10.6 0.8 copy.17
  11.4 0.0 copy-done.3
  11.4 0.1 copy.15
  11.5 0.1 copy.18
  11.7 0.1 copy.16
  11.8 0.7 pad_maximum_fusion
  12.5 11.0 %shard_map.85 = (f32[16,136,128]{2,1,0:T(8,128)}, f32[16,128,128]{2,1,0:T(8,128)}, bf16[16,128,128]{2,1,0:T(8,128)(2,1)}, bf16[16,128,128]{2,1,0:T(8,128)(2,1)}) custom-call(bf16[2048,128]{1,0:T(8,128)(2,1)} %bitcast.7, bf16[2048,128]{1,0:T(8,128)(2,1)} %bitcast.8, bf16[128,128]{1,0:T(8,128)(2,1)} %get-tuple-element.29.map_ref.mk_ref), custom_call_target="tpu_custom_call" | custom-call | tf_op jit(solution)/shard_map/pallas_call | solution.py:404
  23.5 39.1 %shard_map.86.p_ref = f32[16,136,128]{2,1,0:T(8,128)} custom-call(f32[16,136,128]{2,1,0:T(8,128)} %get-tuple-element.15.x_ref), custom_call_target="tpu_custom_call" | custom-call | tf_op jit(solution)/shard_map/pallas_call | solution.py:404
  62.7 0.0 collective-permute-done.1
  62.7 0.0 copy-start.1
  62.7 0.0 collective-permute-done
  62.7 0.0 copy-start.2
  62.7 0.7 copy-done.1
  63.4 0.1 copy-done.2
  63.5 35.0 %shard_map.87 = (bf16[2048,128]{1,0:T(8,128)(2,1)}, f32[16,136,128]{2,1,0:T(8,128)}, f32[128,128]{1,0:T(8,128)}, f32[16,128,128]{2,1,0:T(8,128)}, f32[16,64,128]{2,1,0:T(8,128)}) custom-call(bf16[2048,128]{1,0:T(8,128)(2,1)} %bitcast.9, bf16[2048,128]{1,0:T(8,128)(2,1)} %bitcast.10, bf16[16,128,128]{2,1,0:T(8,128)(2,1)} %get-tuple-element.12.k_ref, ...), custom_call_target="tpu_custom_call" | custom-call | tf_op jit(solution)/shard_map/pallas_call | solution.py:404
  98.5 1.3 collective-permute-start.2
  99.8 50.8 %shard_map.88.later_ref = f32[16,136,128]{2,1,0:T(8,128)} custom-call(f32[16,136,128]{2,1,0:T(8,128)} %get-tuple-element.17.x_ref), custom_call_target="tpu_custom_call" | custom-call | tf_op jit(solution)/shard_map/pallas_call | solution.py:404
  150.6 0.0 collective-permute-done.2.back_ref
  150.6 0.0 copy-start
  150.6 0.8 copy-done
  151.4 10.5 %shard_map.89.x_ref = f32[128,128]{1,0:T(8,128)} custom-call(f32[16,136,128]{2,1,0:T(8,128)} %shard_map.88.later_ref, f32[16,128,128]{2,1,0:T(8,128)} %get-tuple-element.18.near_ref, f32[16,64,128]{2,1,0:T(8,128)} %copy-done, bf16[16,128,128]{2,1,0:T(8,128)(2,1)} %get-tuple-element.12.k_ref, bf16[16,128,128]{2,1,0:T(8,128)(2,1)} %get-tuple-element.13.v_ref, ...), custom_call_target="tpu_custom_call" | custom-call | tf_op jit(solution)/shard_map/pallas_call | solution.py:404
  161.9 24.3 %shard_map.90 = f32[128,128]{1,0:T(8,128)} custom-call(f32[128,128]{1,0:T(8,128)} %shard_map.89.x_ref), custom_call_target="tpu_custom_call" | custom-call | tf_op jit(solution)/shard_map/pallas_call | solution.py:404
  186.2 1.0 fusion
  187.2 0.7 copy.20
  187.9 0.7 copy.19
  (1 shorter events, 0.0 us)
Async XLA Ops:
  0.6 10.8 %copy-start.3 = (bf16[128,64]{0,1:T(8,128)(2,1)S(1)}, bf16[128,64]{0,1:T(8,128)(2,1)}, u32[]{:S(2)}) copy-start(bf16[128,64]{0,1:T(8,128)(2,1)} %param.11) | copy-start | bytes 49156
  1.6 61.0 %collective-permute-start.1 = (bf16[64,16,128]{2,1,0:T(8,128)(2,1)S(1)}, bf16[64,16,128]{2,1,0:T(8,128)(2,1)S(1)}, u32[]{:S(2)}, u32[]{:S(2)}) collective-permute-start(bf16[64,16,128]{2,1,0:T(8,128)(2,1)S(1)} %slice.13), channel_id=1, source_target_pairs={{0,2},{2,4},{4,6},{6,8},{8,10},{10,12},{12,14},{14,16},{16,18},{18... | collective-permute-start | bytes 786440 | tf_op jit(solution)/shard_map/ppermute | solution.py:452
  6.6 56.0 %collective-permute-start = (bf16[64,16,128]{2,1,0:T(8,128)(2,1)S(1)}, bf16[64,16,128]{2,1,0:T(8,128)(2,1)S(1)}, u32[]{:S(2)}, u32[]{:S(2)}) collective-permute-start(bf16[64,16,128]{2,1,0:T(8,128)(2,1)S(1)} %slice.12), channel_id=1, source_target_pairs={{0,2},{2,4},{4,6},{6,8},{8,10},{10,12},{12,14},{14,16},{16,18},{18... | collective-permute-start | bytes 786440 | tf_op jit(solution)/shard_map/ppermute | solution.py:452
  62.7 0.7 copy-start.1
  62.7 0.8 copy-start.2
  98.5 52.1 %collective-permute-start.2 = (f32[16,64,128]{2,1,0:T(8,128)}, f32[16,64,128]{2,1,0:T(8,128)S(1)}, u32[]{:S(2)}, u32[]{:S(2)}) collective-permute-start(f32[16,64,128]{2,1,0:T(8,128)} %get-tuple-element.19), channel_id=1, source_target_pairs={{2,0},{4,2},{6,4},{8,6},{10,8},{12,10},{14,12},{16,14},{18,16},{20... | collective-permute-start | bytes 1572872 | tf_op jit(solution)/shard_map/ppermute | solution.py:452
  150.6 0.8 copy-start

commit v2 on v0

v2 whole, which is shorter than its diff:
```python
import functools

import jax
import jax.numpy as jnp
from jax import lax
from jax.experimental import pallas as pl
from jax.experimental.pallas import tpu as pltpu
from jax.sharding import PartitionSpec as P

WINDOW = 64
FEAT = 64
PLANE = 16
ROWS = 136
MESH = pl.DeviceIdType.MESH
F32 = jnp.float32
BF16 = jnp.bfloat16
VMEM_LIMIT = 56 * 1024 * 1024


def dot_nn(a, b):
    return lax.dot_general(a, b, (((1,), (0,)), ((), ())), preferred_element_type=F32)


def dot_nt(a, b):
    return lax.dot_general(a, b, (((1,), (1,)), ((), ())), preferred_element_type=F32)


def dot_tn(a, b):
    return lax.dot_general(a, b, (((0,), (0,)), ((), ())), preferred_element_type=F32)


def split(x):
    high = x.astype(BF16)
    return high, (x - high.astype(F32)).astype(BF16)


def left_half(shape):
    return lax.broadcasted_iota(jnp.int32, shape, len(shape) - 1) < FEAT


def features(x, pair_map):
    hidden = dot_nn(x, pair_map)
    left = left_half(hidden.shape)
    top_left = jnp.max(jnp.where(left, hidden, -jnp.inf), -1, keepdims=True)
    top_right = jnp.max(jnp.where(left, -jnp.inf, hidden), -1, keepdims=True)
    e = jnp.exp(hidden - jnp.where(left, top_left, top_right))
    sum_left = jnp.sum(jnp.where(left, e, 0.0), -1, keepdims=True)
    sum_right = jnp.sum(jnp.where(left, 0.0, e), -1, keepdims=True)
    return e * jnp.where(left, 1.0 / sum_left, 1.0 / sum_right)


def feature_grad(x, soft, upstream):
    left = left_half(soft.shape)
    product = soft * upstream
    inner_left = jnp.sum(jnp.where(left, product, 0.0), -1, keepdims=True)
    inner_right = jnp.sum(jnp.where(left, 0.0, product), -1, keepdims=True)
    part = soft * (upstream - jnp.where(left, inner_left, inner_right))
    u = part - pltpu.roll(part, FEAT, 1)
    return dot_tn(x, u.astype(BF16))


def head_rows(ref, head, rows, heads):
    return ref[pl.ds(head, rows, stride=heads), :]


def widen(src, dst):
    dst[...] = src[...].astype(F32)


class Scan:
    def __init__(self, x, parts, totals, result, sems, reverse):
        self.x, self.parts, self.totals, self.result, self.reverse = x, parts, totals, result, reverse
        self.send_up, self.recv_up, self.send_z, self.recv_z, self.send_down, self.recv_down = sems
        me = lax.axis_index("seq")
        self.layers = lax.axis_size("seq") // PLANE
        self.z, self.p = me // PLANE, me % PLANE

    def in_plane(self, k):
        return {"seq": self.z * PLANE + k}

    def up(self, k, into):
        return pltpu.make_async_remote_copy(
            src_ref=self.x.at[k], dst_ref=self.parts.at[into],
            send_sem=self.send_up.at[k], recv_sem=self.recv_up.at[into],
            device_id=self.in_plane(k), device_id_type=MESH,
        )

    def down(self, k, into):
        return pltpu.make_async_remote_copy(
            src_ref=self.parts.at[k], dst_ref=self.result.at[into],
            send_sem=self.send_down.at[k], recv_sem=self.recv_down.at[into],
            device_id=self.in_plane(k), device_id_type=MESH,
        )

    def across(self, i, to):
        other = (self.z + i) % self.layers
        into = self.z if to else other
        return pltpu.make_async_remote_copy(
            src_ref=self.totals.at[self.z], dst_ref=self.totals.at[into],
            send_sem=self.send_z.at[other], recv_sem=self.recv_z.at[into],
            device_id={"seq": other * PLANE + self.p}, device_id_type=MESH,
        )

    def give(self, head):
        @pl.when(head != self.p)
        def _():
            self.up(head, self.p).start()

        @pl.when(head == self.p)
        def _():
            self.parts[head] = self.x[head]

    def collect(self):
        def gather(i, total):
            k = PLANE - 1 - i if self.reverse else i

            @pl.when(k != self.p)
            def _():
                self.up(k, k).wait_recv()

            part = self.parts[k]
            self.parts[k] = total
            return total + part

        self.totals[self.z] = lax.fori_loop(0, PLANE, gather, jnp.zeros(self.x.shape[1:], F32))
        for i in range(1, self.layers):
            self.across(i, True).start()

    def spread(self):
        for i in range(1, self.layers):
            self.across(i, False).wait_recv()
        base = jnp.zeros(self.x.shape[1:], F32)
        for k in range(self.layers):
            reached = k > self.z if self.reverse else k < self.z
            base = base + jnp.where(reached, self.totals[k], 0.0)

        def start(i, carry):
            to = (self.p + i) % PLANE
            self.parts[to] = self.parts[to] + base
            self.down(to, self.p).start()
            return carry

        lax.fori_loop(1, PLANE, start, 0)
        self.result[self.p] = self.parts[self.p] + base

    def receive(self, head):
        @pl.when(head != self.p)
        def _():
            self.down(head, head).wait_recv()

    def finish(self):
        def wait(i, carry):
            k = (self.p + i) % PLANE
            self.down(k, k).wait_send()
            self.up(k, k).wait_send()
            return carry

        lax.fori_loop(1, PLANE, wait, 0)
        for i in range(1, self.layers):
            self.across(i, True).wait_send()


class Total:
    def __init__(self, x, out, parts, totals, sems):
        self.x, self.out, self.parts, self.totals = x, out, parts, totals
        self.send1, self.recv1, self.send_z, self.recv_z, self.send2, self.recv2 = sems
        me, core = lax.axis_index("seq"), lax.axis_index("head")
        self.cores = lax.axis_size("head")
        self.others = lax.axis_size("seq") // PLANE * self.cores
        self.z, self.p = me // PLANE, me % PLANE
        self.here = self.z * self.cores + core
        self.rows = x.shape[0] // PLANE

    def rows_of(self, k):
        return pl.ds(pl.multiple_of(k * self.rows, self.rows), self.rows)

    def beyond(self, i):
        at = (self.here + i) % self.others
        return at, {"seq": (at // self.cores) * PLANE + self.p, "head": at % self.cores}

    def up(self, k, into):
        return pltpu.make_async_remote_copy(
            src_ref=self.x.at[self.rows_of(k)], dst_ref=self.parts.at[into],
            send_sem=self.send1.at[k], recv_sem=self.recv1.at[into],
            device_id={"seq": self.z * PLANE + k}, device_id_type=MESH,
        )

    def across(self, i, to):
        at, device = self.beyond(i)
        into = self.here if to else at
        return pltpu.make_async_remote_copy(
            src_ref=self.totals.at[self.here], dst_ref=self.totals.at[into],
            send_sem=self.send_z.at[at], recv_sem=self.recv_z.at[into],
            device_id=device, device_id_type=MESH,
        )

    def down(self, k, into):
        return pltpu.make_async_remote_copy(
            src_ref=self.out.at[self.rows_of(self.p)], dst_ref=self.out.at[self.rows_of(into)],
            send_sem=self.send2.at[k], recv_sem=self.recv2.at[into],
            device_id={"seq": self.z * PLANE + k}, device_id_type=MESH,
        )

    def give(self):
        def start(i, carry):
            self.up((self.p + i) % PLANE, self.p).start()
            return carry

        lax.fori_loop(1, PLANE, start, 0)
        self.parts[self.p] = self.x[self.rows_of(self.p)]

    def collect(self):
        def gather(k, total):
            @pl.when(k != self.p)
            def _():
                self.up(k, k).wait_recv()

            return total + self.parts[k]

        zero = jnp.zeros((self.rows, self.x.shape[1]), F32)
        self.totals[self.here] = lax.fori_loop(0, PLANE, gather, zero)

        def start(i, carry):
            self.across(i, True).start()
            return carry

        lax.fori_loop(1, self.others, start, 0)

    def spread(self):
        def wait(i, carry):
            self.across(i, False).wait_recv()
            return carry

        lax.fori_loop(1, self.others, wait, 0)
        result = self.totals[0]
        for k in range(1, self.others):
            result = result + self.totals[k]
        self.out[self.rows_of(self.p)] = result

        def start(i, carry):
            self.down((self.p + i) % PLANE, self.p).start()
            return carry

        lax.fori_loop(1, PLANE, start, 0)

    def finish(self):
        def wait(i, carry):
            k = (self.p + i) % PLANE
            self.down(k, k).wait_recv()
            self.down(k, k).wait_send()
            self.up(k, k).wait_send()
            return carry

        lax.fori_loop(1, PLANE, wait, 0)

        def wait_across(i, carry):
            self.across(i, False).wait_send()
            return carry

        lax.fori_loop(1, self.others, wait_across, 0)


def greet():
    me, core = lax.axis_index("seq"), lax.axis_index("head")
    count, cores = lax.axis_size("seq"), lax.axis_size("head")
    others = count // PLANE * cores
    z, p = me // PLANE, me % PLANE
    barrier = pltpu.get_barrier_semaphore()

    def plane(i, carry):
        device = {"seq": z * PLANE + (p + i) % PLANE}
        pl.semaphore_signal(barrier, inc=1, device_id=device, device_id_type=MESH)
        return carry

    def beyond(i, carry):
        at = (z * cores + core + i) % others
        device = {"seq": (at // cores) * PLANE + p, "head": at % cores}
        pl.semaphore_signal(barrier, inc=1, device_id=device, device_id_type=MESH)
        return carry

    lax.fori_loop(1, PLANE, plane, 0)
    lax.fori_loop(1, others, beyond, 0)
    for other in ((me + 1) % count, (me + count - 1) % count):
        pl.semaphore_signal(barrier, inc=1, device_id={"seq": other}, device_id_type=MESH)
    pl.semaphore_wait(barrier, PLANE - 1 + others - 1 + 2)


def kernel(
    heads, total_tokens, q_ref, k_ref, v_ref, t_ref, mq_ref, mk_ref, out_ref, grad_ref,
    q_wide, k_wide, v_wide, t_wide, out_wide, halo, hk_wide, hv_wide,
    ext_k, ext_v, ext_phi, q_heads, soft_q, soft_k, numer_near, denom_near, damp, halo_state, halo_sum,
    d_numer_all, d_denom_all, first_grad, first_sum, near, back, back_in,
    x1, parts1, totals1, prior, x2, parts2, totals2, later, gq, gk, packed, parts3, totals3,
    send_halo, recv_halo, send_back, recv_back, *sems,
):
    w = WINDOW
    rows = 2 * w
    me, count = lax.axis_index("seq"), lax.axis_size("seq")
    p = me % PLANE
    has_prior = me > 0
    has_later = me < count - 1
    forward = Scan(x1, parts1, totals1, prior, sems[0:6], False)
    backward = Scan(x2, parts2, totals2, later, sems[6:12], True)
    final = Total(packed, grad_ref, parts3, totals3, sems[12:18])
    greet()

    def halo_copy(i, ref):
        return pltpu.make_async_remote_copy(
            src_ref=ref.at[pl.ds(w * heads, w * heads)], dst_ref=halo.at[i],
            send_sem=send_halo.at[i], recv_sem=recv_halo.at[i],
            device_id={"seq": (me + 1) % count}, device_id_type=MESH,
        )

    def back_copy(pair):
        return pltpu.make_async_remote_copy(
            src_ref=back.at[pl.ds(2 * pair, 2)], dst_ref=back_in.at[pl.ds(2 * pair, 2)],
            send_sem=send_back.at[pair], recv_sem=recv_back.at[pair],
            device_id={"seq": (me + count - 1) % count}, device_id_type=MESH,
        )

    @pl.when(has_later)
    def _():
        halo_copy(0, k_ref).start()
        halo_copy(1, v_ref).start()

    widen(k_ref, k_wide)
    widen(v_ref, v_wide)
    map_q, map_k = mq_ref[...], mk_ref[...]

    def key_part(i, carry):
        pair = [(p + 2 * i) % PLANE, (p + 2 * i + 1) % PLANE]
        for head in pair:
            k = head_rows(k_wide, head, rows, heads).astype(BF16)
            v = head_rows(v_wide, head, rows, heads).astype(BF16)
            soft = features(k, map_k)
            phi = soft.astype(BF16)
            ext_k[head, w:, :] = k
            ext_v[head, w:, :] = v
            ext_phi[head, w:, :] = phi
            soft_k[head] = soft
            x1[head, :128, :] = dot_tn(phi, v)
            x1[head, 128:, :] = jnp.broadcast_to(jnp.sum(phi.astype(F32), 0, keepdims=True), (ROWS - 128, 128))
        for head in pair:
            forward.give(head)
        return carry

    lax.fori_loop(0, heads // 2, key_part, 0)

    widen(q_ref, q_wide)
    widen(t_ref, t_wide)

    @pl.when(has_prior)
    def _():
        halo_copy(0, k_ref).wait_recv()
        halo_copy(1, v_ref).wait_recv()

    @pl.when(jnp.logical_not(has_prior))
    def _():
        halo[...] = jnp.zeros_like(halo)

    hk_wide[...] = halo[0].astype(F32)
    hv_wide[...] = halo[1].astype(F32)
    row = lax.broadcasted_iota(jnp.int32, (w, rows), 0)
    col = lax.broadcasted_iota(jnp.int32, (w, rows), 1)
    scale = 128 ** (-0.5)

    def masks(c):
        in_window = (col > row) & (col <= row + w)
        in_far = col <= row
        if c:
            return in_window, in_far
        live = (col >= w) | has_prior
        return in_window & live, in_far & live

    def near_part(i, carry):
        for head in (2 * i, 2 * i + 1):
            hk = head_rows(hk_wide, head, w, heads).astype(BF16)
            hv = head_rows(hv_wide, head, w, heads).astype(BF16)
            phi_h = jnp.where(has_prior, features(hk, map_k), 0.0).astype(BF16)
            ext_k[head, :w, :] = hk
            ext_v[head, :w, :] = hv
            ext_phi[head, :w, :] = phi_h
            halo_state[head] = dot_tn(phi_h, hv)
            halo_sum[head] = jnp.broadcast_to(jnp.sum(phi_h.astype(F32), 0, keepdims=True), (8, 128))
            q = head_rows(q_wide, head, rows, heads).astype(BF16)
            q_heads[head] = q
            soft = features(q, map_q)
            soft_q[head] = soft
            phi_q = soft.astype(BF16)
            for c in range(2):
                block, span = pl.ds(c * w, w), pl.ds(c * w, rows)
                in_window, in_far = masks(c)
                scores = dot_nt(q[c * w : (c + 1) * w], ext_k[head, span, :]) * scale
                scores = jnp.where(in_window, scores, -jnp.inf)
                top = jnp.max(scores, -1, keepdims=True)
                damping = jnp.exp(-top)
                far = damping * dot_nt(phi_q[c * w : (c + 1) * w], ext_phi[head, span, :])
                weight = jnp.exp(scores - top) + jnp.where(in_far, far, 0.0)
                numer_near[head, block, :] = dot_nn(weight.astype(BF16), ext_v[head, span, :])
                denom_near[head, block, :] = jnp.sum(weight, -1, keepdims=True)
                damp[head, block, :] = damping

        @pl.when(i == 4)
        def _():
            forward.collect()

        @pl.when(i == 6)
        def _():
            forward.spread()

        return carry

    lax.fori_loop(0, heads // 2, near_part, 0)

    def states(head):
        one = prior[head, :128, :]
        zero = one - halo_state[head]
        sum_one = prior[head, 128:129, :]
        return (zero, one), (sum_one - halo_sum[head, 0:1, :], sum_one)

    def middle_part(i, carry):
        pair = [(p + 2 * PLANE - 2 * i) % PLANE, (p + 2 * PLANE - 2 * i - 1) % PLANE]
        for head in pair:
            forward.receive(head)
        for head in pair:
            state, ksum = states(head)
            phi_q = soft_q[head].astype(BF16)
            grads = []
            for c in range(2):
                block = pl.ds(c * w, w)
                pq = phi_q[c * w : (c + 1) * w]
                wide_pq = pq.astype(F32)
                damping = damp[head, block, :]
                high, low = split(state[c])
                state_den = jnp.sum(wide_pq * ksum[c], -1, keepdims=True)
                numer = numer_near[head, block, :] + damping * (dot_nn(pq, high) + dot_nn(pq, low))
                inverse = 1.0 / (denom_near[head, block, :] + damping * state_den)
                output = numer * inverse
                at = pl.ds(c * w * heads + head, w, stride=heads)
                out_wide[at, :] = output
                d_out = (output - t_wide[at, :]) * (2.0 / total_tokens)
                d_numer = d_out * inverse
                d_denom = -jnp.sum(d_out * output, -1, keepdims=True) * inverse
                d_numer_all[head, block, :] = d_numer
                d_denom_all[head, block, :] = d_denom
                g_state = dot_tn(pq, (damping * d_numer).astype(BF16))
                g_sum = jnp.sum(damping * d_denom * wide_pq, 0, keepdims=True)
                grads.append((g_state, g_sum))
            first_grad[head] = grads[0][0]
            first_sum[head] = jnp.broadcast_to(grads[0][1], (8, 128))
            x2[head, :128, :] = grads[0][0] + grads[1][0]
            x2[head, 128:, :] = jnp.broadcast_to(grads[0][1] + grads[1][1], (ROWS - 128, 128))
        for head in pair:
            backward.give(head)
        return carry

    lax.fori_loop(0, heads // 2, middle_part, 0)
    gq[...] = jnp.zeros_like(gq)
    gk[...] = jnp.zeros_like(gk)

    def far_part(i, carry):
        for head in (2 * i, 2 * i + 1):
            state, ksum = states(head)
            soft = soft_q[head]
            phi_q = soft.astype(BF16)
            d_phi, d_near = [], []
            for c in range(2):
                block, span = pl.ds(c * w, w), pl.ds(c * w, rows)
                in_far = masks(c)[1]
                damping = damp[head, block, :]
                d_numer = d_numer_all[head, block, :]
                d_denom = d_denom_all[head, block, :]
                high, low = split(state[c])
                dn_high, dn_low = split(d_numer)
                d_weight = dot_nt(dn_high, ext_v[head, span, :]) + d_denom
                far_grad = jnp.where(in_far, damping * d_weight, 0.0).astype(BF16)
                through = dot_nt(dn_high, high) + dot_nt(dn_high, low) + dot_nt(dn_low, high)
                d_phi.append(dot_nn(far_grad, ext_phi[head, span, :]) + damping * (through + d_denom * ksum[c]))
                d_near.append(dot_tn(far_grad, phi_q[c * w : (c + 1) * w]))
            high, low = split(first_grad[head])
            hv = ext_v[head, :w, :]
            back[head] = d_near[0][:w] - (dot_nt(hv, high) + dot_nt(hv, low) + first_sum[head, 0:1, :])
            near[head, :w, :] = d_near[0][w:] + d_near[1][:w]
            near[head, w:, :] = d_near[1][w:]
            gq[...] += feature_grad(q_heads[head], soft, jnp.concatenate(d_phi, 0))

        @pl.when(has_prior)
        def _():
            back_copy(i).start()

        @pl.when(i == 2)
        def _():
            backward.collect()

        @pl.when(i == 4)
        def _():
            backward.spread()

        return carry

    lax.fori_loop(0, heads // 2, far_part, 0)
    out_ref[...] = out_wide[...].astype(BF16)

    @pl.when(has_later)
    def _():
        def wait(i, carry):
            back_copy(i).wait_recv()
            return carry

        lax.fori_loop(0, heads // 2, wait, 0)

    @pl.when(jnp.logical_not(has_later))
    def _():
        back_in[...] = jnp.zeros_like(back_in)

    def last_part(i, carry):
        pair = [(p + 2 * PLANE - 2 * i) % PLANE, (p + 2 * PLANE - 2 * i - 1) % PLANE]
        for head in pair:
            backward.receive(head)
        for head in pair:
            v, k = ext_v[head, w:, :], ext_k[head, w:, :]
            high, low = split(later[head, :128, :])
            d_near = near[head]
            d_near = jnp.concatenate([d_near[:w], d_near[w:] + back_in[head]], 0)
            d_phi = d_near + dot_nt(v, high) + dot_nt(v, low) + later[head, 128:129, :]
            gk[...] += feature_grad(k, soft_k[head], d_phi)
        return carry

    lax.fori_loop(0, heads // 2, last_part, 0)
    packed[...] = jnp.where(left_half(packed.shape), gq[...], -gk[...])
    final.give()
    final.collect()
    final.spread()
    final.finish()
    forward.finish()
    backward.finish()

    @pl.when(has_later)
    def _():
        halo_copy(0, k_ref).wait_send()
        halo_copy(1, v_ref).wait_send()

    @pl.when(has_prior)
    def _():
        def wait(i, carry):
            back_copy(i).wait_send()
            return carry

        lax.fori_loop(0, heads // 2, wait, 0)


def per_device(queries, keys, values, target, map_q, map_k):
    rows, heads, size = queries.shape
    total_tokens = rows * lax.axis_size("seq")
    layers = lax.axis_size("seq") // PLANE
    others = layers * lax.axis_size("head")
    flat = (rows * heads, size)
    half = (WINDOW * heads, size)
    wide = pltpu.VMEM(flat, F32)
    tiles = pltpu.VMEM((heads, rows, size), F32)
    halves = pltpu.VMEM((heads, WINDOW, size), F32)
    ext = pltpu.VMEM((heads, rows + WINDOW, size), BF16)
    column = pltpu.VMEM((heads, rows, 1), F32)
    row = pltpu.VMEM((heads, 8, size), F32)
    square = pltpu.VMEM((heads, size, size), F32)
    slices = pltpu.VMEM((heads, ROWS, size), F32)
    layer = pltpu.VMEM((layers, ROWS, size), F32)
    grad = pltpu.VMEM((size, size), F32)
    dma = pltpu.SemaphoreType.DMA
    in_plane, scan_z, sum_z = dma((PLANE,)), dma((layers,)), dma((others,))
    scan_sems = [in_plane, in_plane, scan_z, scan_z, in_plane, in_plane]
    pair_q = jnp.concatenate([map_q, -map_q], 1)
    pair_k = jnp.concatenate([map_k, -map_k], 1)
    vmem = pl.BlockSpec(memory_space=pltpu.VMEM)
    hybrid, grads = pl.pallas_call(
        functools.partial(kernel, heads, total_tokens),
        out_shape=[jax.ShapeDtypeStruct(flat, BF16), jax.ShapeDtypeStruct((size, size), F32)],
        in_specs=[vmem] * 6,
        out_specs=[vmem] * 2,
        scratch_shapes=[
            wide, wide, wide, wide, wide, pltpu.VMEM((2,) + half, BF16), pltpu.VMEM(half, F32), pltpu.VMEM(half, F32),
            ext, ext, ext, pltpu.VMEM((heads, rows, size), BF16), tiles, tiles, tiles, column, column, square, row,
            tiles, column, square, row, tiles, halves, halves,
            slices, slices, layer, slices, slices, slices, layer, slices, grad, grad, grad,
            pltpu.VMEM((PLANE, size // PLANE, size), F32), pltpu.VMEM((others, size // PLANE, size), F32),
            dma((2,)), dma((2,)), dma((heads // 2,)), dma((heads // 2,)),
            *scan_sems, *scan_sems, in_plane, in_plane, sum_z, sum_z, in_plane, in_plane,
        ],
        compiler_params=pltpu.CompilerParams(vmem_limit_bytes=VMEM_LIMIT, collective_id=0, has_side_effects=True),
    )(queries.reshape(flat), keys.reshape(flat), values.reshape(flat), target.reshape(flat), pair_q, pair_k)
    return hybrid.reshape(rows, heads, size), grads[:, :FEAT], grads[:, FEAT:]


def solution(mesh):
    tokens = P("seq", "head", None)
    return jax.shard_map(
        per_device,
        mesh=mesh,
        in_specs=(tokens, tokens, tokens, tokens, P(), P()),
        out_specs=(tokens, P(), P()),
        check_vma=False,
    )
```

time: 1040 us -> 132 us (0.13)
  waiting for transfers between devices: 338 us -> 0 us
  blocking collectives: 322 us -> 0 us
  other arithmetic: 261 us -> 1.46 us
  Pallas kernels: 0 us -> 123 us
  local copies, waits for them, and re-layouts: 55.8 us -> 5.92 us
  matrix products: 31.6 us -> 0 us
  between operations: 14.5 us -> 0.66 us
    all_gather x2 -> x0, blocking collectives: 322 us -> none  [prefix(): everything = jax.tree.map(lambda part: lax.all_gather(part, axis), array)]
    select_n x257 -> x0, other arithmetic: 249 us -> none  [the longest x256 249 us: turn(): return jax.tree.map(lambda a, b: jnp.where(reached, a, b), new, before)]
    all_gather x2 -> x0, waiting for transfers between devices: 192 us -> none  [prefix(): everything = jax.tree.map(lambda part: lax.all_gather(part, axis), array)]
    psum x1 -> x0, waiting for transfers between devices: 140 us -> none  [per_device(): summed_q, summed_k = lax.psum((grad_q, grad_k), ('seq', 'head'))]
    pallas_call x0 -> x1, Pallas kernels: none -> 123 us  [per_device(): pl.pallas_call(functools.partial(kernel, heads, total_tokens), out_shape=...]
    dot_general x15 -> x0, matrix products: 24.2 us -> none  [the longest x2 5 us: feature_grad(): jnp.einsum('thd,thf->df', inputs, inner_grad.astype(jnp.bfloat16), prefer...]
    concatenate x11 -> x0, local copies, waits for them, and re-layouts: 15.2 us -> none  [the longest x8 14.2 us: feature_map(): jnp.concatenate([upper_soft, lower_soft], -1).astype(jnp.bfloat16)]
    slice x17 -> x1, local copies, waits for them, and re-layouts: 15.8 us -> 0.99 us  [per_device(): return (hybrid.reshape(rows, heads, size), grads[:, :FEAT], grads[:, FEAT:])]
  transfers between devices with their start and end apart: 6 -> 0, of which waited for: 5 -> 0; matrix products, arithmetic and copies ran while one was open for 6% -> 0% of each run, Pallas kernels for 0% -> 0%
where the time goes in v2:
time: 132 us; the launch traced here: 131 us
  Pallas kernels  123 us (93%)
  local copies, waits for them, and re-layouts  5.92 us (4%)
  other arithmetic  1.46 us (1%)
    pallas_call x1, Pallas kernels, per_device(): pl.pallas_call(functools.partial(kernel, heads, total_tokens), out_shape=...  123 us
    unnamed x9, local copies, waits for them, and re-layouts  4.7 us

profile of v2, /device:TPU:1, one launch (start us, length us, event | category | flops | bytes accessed | tf_op | source)
XLA Modules:
  0.0 131.5 jit_solution(8080437482320929205)
XLA Ops:
  0.6 0.7 neg.6
  1.4 0.0 copy-start.1
  1.4 0.1 copy.16
  1.5 0.6 copy-done.1
  2.1 0.0 copy-start
  2.1 0.1 copy.18
  2.2 0.6 copy-done
  2.8 0.1 copy.15
  2.9 0.1 copy.17
  3.0 0.7 pad_maximum_fusion
  3.8 123.4 %shard_map.85 = (bf16[2048,128]{1,0:T(8,128)(2,1)}, f32[128,128]{1,0:T(8,128)}) custom-call(bf16[2048,128]{1,0:T(8,128)(2,1)} %bitcast.6, bf16[2048,128]{1,0:T(8,128)(2,1)} %bitcast.7, bf16[2048,128]{1,0:T(8,128)(2,1)} %bitcast.8, bf16[2048,128]{1,0:T(8,128)(2,1)} %bitcast.9, bf16[128,128]{1,0:T(8,128)(2,1)} %get-tuple-element.15.mq_ref, ...), custom_call_target="tpu_custom_call" | custom-call | tf_op jit(solution)/shard_map/pallas_call | solution.py:575
  127.2 1.0 fusion
  128.2 0.7 copy.20
  128.9 0.7 copy.19
  129.6 1.9 %copy.22 = bf16[128,16,128]{2,1,0:T(8,128)(2,1)} copy(bf16[128,16,128]{2,1,0:T(8,128)(2,1)} %bitcast.5) | data formatting | bytes 1048576
  (1 shorter events, 0.0 us)
Async XLA Ops:
  1.4 0.7 copy-start.1
  2.1 0.7 copy-start

commit v3 on v2

--- a/solution.py
+++ b/solution.py
@@ -39,7 +39,7 @@
 
 
 def features(x, pair_map):
-    hidden = dot_nn(x, pair_map)
+    hidden = dot_nt(x, pair_map)
     left = left_half(hidden.shape)
     top_left = jnp.max(jnp.where(left, hidden, -jnp.inf), -1, keepdims=True)
     top_right = jnp.max(jnp.where(left, -jnp.inf, hidden), -1, keepdims=True)
@@ -56,7 +56,7 @@
     inner_right = jnp.sum(jnp.where(left, 0.0, product), -1, keepdims=True)
     part = soft * (upstream - jnp.where(left, inner_left, inner_right))
     u = part - pltpu.roll(part, FEAT, 1)
-    return dot_tn(x, u.astype(BF16))
+    return dot_tn(u.astype(BF16), x)
 
 
 def head_rows(ref, head, rows, heads):
@@ -65,6 +65,14 @@
 
 def widen(src, dst):
     dst[...] = src[...].astype(F32)
+
+
+def wrapped(k, count):
+    return jnp.where(k >= count, k - count, k)
+
+
+def await_bytes(ref, sem):
+    pltpu.make_async_copy(ref, ref, sem).wait()
 
 
 class Scan:
@@ -78,64 +86,52 @@
     def in_plane(self, k):
         return {"seq": self.z * PLANE + k}
 
-    def up(self, k, into):
-        return pltpu.make_async_remote_copy(
-            src_ref=self.x.at[k], dst_ref=self.parts.at[into],
-            send_sem=self.send_up.at[k], recv_sem=self.recv_up.at[into],
-            device_id=self.in_plane(k), device_id_type=MESH,
-        )
+    def give(self, head):
+        @pl.when(head != self.p)
+        def _():
+            pltpu.make_async_remote_copy(
+                src_ref=self.x.at[head], dst_ref=self.parts.at[self.p], send_sem=self.send_up, recv_sem=self.recv_up,
+                device_id=self.in_plane(head), device_id_type=MESH,
+            ).start()
+
+        @pl.when(head == self.p)
+        def _():
+            pltpu.make_async_copy(self.x.at[head], self.parts.at[self.p], self.recv_up).start()
+
+    def collect(self):
+        await_bytes(self.parts, self.recv_up)
+
+        def gather(i, total):
+            k = PLANE - 1 - i if self.reverse else i
+            part = self.parts[k]
+            self.parts[k] = total
+            return total + part
+
+        self.totals[self.z] = lax.fori_loop(0, PLANE, gather, jnp.zeros(self.x.shape[1:], F32))
+        for i in range(1, self.layers):
+            other = wrapped(self.z + i, self.layers)
+            pltpu.make_async_remote_copy(
+                src_ref=self.totals.at[self.z], dst_ref=self.totals.at[self.z],
+                send_sem=self.send_z, recv_sem=self.recv_z,
+                device_id={"seq": other * PLANE + self.p}, device_id_type=MESH,
+            ).start()
 
     def down(self, k, into):
         return pltpu.make_async_remote_copy(
             src_ref=self.parts.at[k], dst_ref=self.result.at[into],
-            send_sem=self.send_down.at[k], recv_sem=self.recv_down.at[into],
+            send_sem=self.send_down, recv_sem=self.recv_down.at[into],
             device_id=self.in_plane(k), device_id_type=MESH,
         )
 
-    def across(self, i, to):
-        other = (self.z + i) % self.layers
-        into = self.z if to else other
-        return pltpu.make_async_remote_copy(
-            src_ref=self.totals.at[self.z], dst_ref=self.totals.at[into],
-            send_sem=self.send_z.at[other], recv_sem=self.recv_z.at[into],
-            device_id={"seq": other * PLANE + self.p}, device_id_type=MESH,
-        )
-
-    def give(self, head):
-        @pl.when(head != self.p)
-        def _():
-            self.up(head, self.p).start()
-
-        @pl.when(head == self.p)
-        def _():
-            self.parts[head] = self.x[head]
-
-    def collect(self):
-        def gather(i, total):
-            k = PLANE - 1 - i if self.reverse else i
-
-            @pl.when(k != self.p)
-            def _():
-                self.up(k, k).wait_recv()
-
-            part = self.parts[k]
-            self.parts[k] = total
-            return total + part
-
-        self.totals[self.z] = lax.fori_loop(0, PLANE, gather, jnp.zeros(self.x.shape[1:], F32))
-        for i in range(1, self.layers):
-            self.across(i, True).start()
-
     def spread(self):
-        for i in range(1, self.layers):
-            self.across(i, False).wait_recv()
+        await_bytes(self.totals.at[pl.ds(0, self.layers - 1)], self.recv_z)
         base = jnp.zeros(self.x.shape[1:], F32)
         for k in range(self.layers):
             reached = k > self.z if self.reverse else k < self.z
             base = base + jnp.where(reached, self.totals[k], 0.0)
 
         def start(i, carry):
-            to = (self.p + i) % PLANE
+            to = wrapped(self.p + i, PLANE)
             self.parts[to] = self.parts[to] + base
             self.down(to, self.p).start()
             return carry
@@ -149,15 +145,10 @@
             self.down(head, head).wait_recv()
 
     def finish(self):
-        def wait(i, carry):
-            k = (self.p + i) % PLANE
-            self.down(k, k).wait_send()
-            self.up(k, k).wait_send()
-            return carry
-
-        lax.fori_loop(1, PLANE, wait, 0)
-        for i in range(1, self.layers):
-            self.across(i, True).wait_send()
+        most = pl.ds(0, PLANE - 1)
+        await_bytes(self.x.at[most], self.send_up)
+        await_bytes(self.parts.at[most], self.send_down)
+        await_bytes(self.totals.at[pl.ds(0, self.layers - 1)], self.send_z)
 
 
 class Total:
@@ -169,95 +160,45 @@
         self.others = lax.axis_size("seq") // PLANE * self.cores
         self.z, self.p = me // PLANE, me % PLANE
         self.here = self.z * self.cores + core
-        self.rows = x.shape[0] // PLANE
-
-    def rows_of(self, k):
-        return pl.ds(pl.multiple_of(k * self.rows, self.rows), self.rows)
-
-    def beyond(self, i):
-        at = (self.here + i) % self.others
-        return at, {"seq": (at // self.cores) * PLANE + self.p, "head": at % self.cores}
-
-    def up(self, k, into):
-        return pltpu.make_async_remote_copy(
-            src_ref=self.x.at[self.rows_of(k)], dst_ref=self.parts.at[into],
-            send_sem=self.send1.at[k], recv_sem=self.recv1.at[into],
-            device_id={"seq": self.z * PLANE + k}, device_id_type=MESH,
-        )
-
-    def across(self, i, to):
-        at, device = self.beyond(i)
-        into = self.here if to else at
-        return pltpu.make_async_remote_copy(
-            src_ref=self.totals.at[self.here], dst_ref=self.totals.at[into],
-            send_sem=self.send_z.at[at], recv_sem=self.recv_z.at[into],
-            device_id=device, device_id_type=MESH,
-        )
-
-    def down(self, k, into):
-        return pltpu.make_async_remote_copy(
-            src_ref=self.out.at[self.rows_of(self.p)], dst_ref=self.out.at[self.rows_of(into)],
-            send_sem=self.send2.at[k], recv_sem=self.recv2.at[into],
-            device_id={"seq": self.z * PLANE + k}, device_id_type=MESH,
-        )
+
+    def in_plane(self, k):
+        return {"seq": self.z * PLANE + k}
 
     def give(self):
-        def start(i, carry):
-            self.up((self.p + i) % PLANE, self.p).start()
-            return carry
-
-        lax.fori_loop(1, PLANE, start, 0)
-        self.parts[self.p] = self.x[self.rows_of(self.p)]
+        for i in range(1, PLANE):
+            to = wrapped(self.p + i, PLANE)
+            pltpu.make_async_remote_copy(
+                src_ref=self.x.at[to], dst_ref=self.parts.at[self.p], send_sem=self.send1, recv_sem=self.recv1,
+                device_id=self.in_plane(to), device_id_type=MESH,
+            ).start()
+        pltpu.make_async_copy(self.x.at[self.p], self.parts.at[self.p], self.recv1).start()
 
     def collect(self):
-        def gather(k, total):
-            @pl.when(k != self.p)
-            def _():
-                self.up(k, k).wait_recv()
-
-            return total + self.parts[k]
-
-        zero = jnp.zeros((self.rows, self.x.shape[1]), F32)
-        self.totals[self.here] = lax.fori_loop(0, PLANE, gather, zero)
-
-        def start(i, carry):
-            self.across(i, True).start()
-            return carry
-
-        lax.fori_loop(1, self.others, start, 0)
+        await_bytes(self.parts, self.recv1)
+        self.totals[self.here] = jnp.sum(self.parts[...], 0)
+        for i in range(1, self.others):
+            at = wrapped(self.here + i, self.others)
+            pltpu.make_async_remote_copy(
+                src_ref=self.totals.at[self.here], dst_ref=self.totals.at[self.here],
+                send_sem=self.send_z, recv_sem=self.recv_z,
+                device_id={"seq": (at // self.cores) * PLANE + self.p, "head": at % self.cores}, device_id_type=MESH,
+            ).start()
 
     def spread(self):
-        def wait(i, carry):
-            self.across(i, False).wait_recv()
-            return carry
-
-        lax.fori_loop(1, self.others, wait, 0)
-        result = self.totals[0]
-        for k in range(1, self.others):
-            result = result + self.totals[k]
-        self.out[self.rows_of(self.p)] = result
-
-        def start(i, carry):
-            self.down((self.p + i) % PLANE, self.p).start()
-            return carry
-
-        lax.fori_loop(1, PLANE, start, 0)
+        await_bytes(self.totals.at[pl.ds(0, self.others - 1)], self.recv_z)
+        self.out[self.p] = jnp.sum(self.totals[...], 0)
+        for i in range(1, PLANE):
+            pltpu.make_async_remote_copy(
+                src_ref=self.out.at[self.p], dst_ref=self.out.at[self.p], send_sem=self.send2, recv_sem=self.recv2,
+                device_id=self.in_plane(wrapped(self.p + i, PLANE)), device_id_type=MESH,
+            ).start()
 
     def finish(self):
-        def wait(i, carry):
-            k = (self.p + i) % PLANE
-            self.down(k, k).wait_recv()
-            self.down(k, k).wait_send()
-            self.up(k, k).wait_send()
-            return carry
-
-        lax.fori_loop(1, PLANE, wait, 0)
-
-        def wait_across(i, carry):
-            self.across(i, False).wait_send()
-            return carry
-
-        lax.fori_loop(1, self.others, wait_across, 0)
+        most = pl.ds(0, PLANE - 1)
+        await_bytes(self.out.at[most], self.recv2)
+        await_bytes(self.out.at[most], self.send2)
+        await_bytes(self.x.at[most], self.send1)
+        await_bytes(self.totals.at[pl.ds(0, self.others - 1)], self.send_z)
 
 
 def greet():
@@ -282,19 +223,26 @@
     lax.fori_loop(1, others, beyond, 0)
     for other in ((me + 1) % count, (me + count - 1) % count):
         pl.semaphore_signal(barrier, inc=1, device_id={"seq": other}, device_id_type=MESH)
-    pl.semaphore_wait(barrier, PLANE - 1 + others - 1 + 2)
+    return PLANE - 1 + others - 1 + 2
 
 
 def kernel(
     heads, total_tokens, q_ref, k_ref, v_ref, t_ref, mq_ref, mk_ref, out_ref, grad_ref,
-    q_wide, k_wide, v_wide, t_wide, out_wide, halo, hk_wide, hv_wide,
+    q_in, k_in, v_in, t_in, q_wide, k_wide, v_wide, t_wide, halo, hk_wide, hv_wide,
     ext_k, ext_v, ext_phi, q_heads, soft_q, soft_k, numer_near, denom_near, damp, halo_state, halo_sum,
     d_numer_all, d_denom_all, first_grad, first_sum, near, back, back_in,
     x1, parts1, totals1, prior, x2, parts2, totals2, later, gq, gk, packed, parts3, totals3,
-    send_halo, recv_halo, send_back, recv_back, *sems,
+    load, send_halo, recv_halo, send_back, recv_back, *sems,
 ):
     w = WINDOW
     rows = 2 * w
+    greeted = greet()
+    loads = [
+        pltpu.make_async_copy(source, target, load.at[i])
+        for i, (source, target) in enumerate([(k_ref, k_in), (v_ref, v_in), (q_ref, q_in), (t_ref, t_in)])
+    ]
+    for copy in loads:
+        copy.start()
     me, count = lax.axis_index("seq"), lax.axis_size("seq")
     p = me % PLANE
     has_prior = me > 0
@@ -302,7 +250,6 @@
     forward = Scan(x1, parts1, totals1, prior, sems[0:6], False)
     backward = Scan(x2, parts2, totals2, later, sems[6:12], True)
     final = Total(packed, grad_ref, parts3, totals3, sems[12:18])
-    greet()
 
     def halo_copy(i, ref):
         return pltpu.make_async_remote_copy(
@@ -318,14 +265,20 @@
             device_id={"seq": (me + count - 1) % count}, device_id_type=MESH,
         )
 
+    loads[0].wait()
+    loads[1].wait()
+    pl.semaphore_wait(pltpu.get_barrier_semaphore(), greeted)
+
     @pl.when(has_later)
     def _():
-        halo_copy(0, k_ref).start()
-        halo_copy(1, v_ref).start()
-
-    widen(k_ref, k_wide)
-    widen(v_ref, v_wide)
-    map_q, map_k = mq_ref[...], mk_ref[...]
+        halo_copy(0, k_in).start()
+        halo_copy(1, v_in).start()
+
+    widen(k_in, k_wide)
+    widen(v_in, v_wide)
+    map_q, map_k = (
+        jnp.concatenate([ref[...], (-ref[...].astype(F32)).astype(BF16)], 0) for ref in (mq_ref, mk_ref)
+    )
 
     def key_part(i, carry):
         pair = [(p + 2 * i) % PLANE, (p + 2 * i + 1) % PLANE]
@@ -346,20 +299,10 @@
 
     lax.fori_loop(0, heads // 2, key_part, 0)
 
-    widen(q_ref, q_wide)
-    widen(t_ref, t_wide)
-
-    @pl.when(has_prior)
-    def _():
-        halo_copy(0, k_ref).wait_recv()
-        halo_copy(1, v_ref).wait_recv()
-
-    @pl.when(jnp.logical_not(has_prior))
-    def _():
-        halo[...] = jnp.zeros_like(halo)
-
-    hk_wide[...] = halo[0].astype(F32)
-    hv_wide[...] = halo[1].astype(F32)
+    loads[2].wait()
+    loads[3].wait()
+    widen(q_in, q_wide)
+    widen(t_in, t_wide)
     row = lax.broadcasted_iota(jnp.int32, (w, rows), 0)
     col = lax.broadcasted_iota(jnp.int32, (w, rows), 1)
     scale = 128 ** (-0.5)
@@ -371,6 +314,41 @@
             return in_window, in_far
         live = (col >= w) | has_prior
         return in_window & live, in_far & live
+
+    def near_block(head, c, q, phi_q):
+        block, span = pl.ds(c * w, w), pl.ds(c * w, rows)
+        in_window, in_far = masks(c)
+        scores = jnp.where(in_window, dot_nt(q, ext_k[head, span, :]) * scale, -jnp.inf)
+        top = jnp.max(scores, -1, keepdims=True)
+        damping = jnp.exp(-top)
+        far = damping * dot_nt(phi_q, ext_phi[head, span, :])
+        weight = jnp.exp(scores - top) + jnp.where(in_far, far, 0.0)
+        numer_near[head, block, :] = dot_nn(weight.astype(BF16), ext_v[head, span, :])
+        denom_near[head, block, :] = jnp.sum(weight, -1, keepdims=True)
+        damp[head, block, :] = damping
+
+    def own_part(i, carry):
+        for head in (2 * i, 2 * i + 1):
+            q = head_rows(q_wide, head, rows, heads).astype(BF16)
+            q_heads[head] = q
+            soft = features(q, map_q)
+            soft_q[head] = soft
+            near_block(head, 1, q[w:], soft[w:].astype(BF16))
+        return carry
+
+    lax.fori_loop(0, heads // 2, own_part, 0)
+
+    @pl.when(has_prior)
+    def _():
+        halo_copy(0, k_in).wait_recv()
+        halo_copy(1, v_in).wait_recv()
+
+    @pl.when(jnp.logical_not(has_prior))
+    def _():
+        halo[...] = jnp.zeros_like(halo)
+
+    hk_wide[...] = halo[0].astype(F32)
+    hv_wide[...] = halo[1].astype(F32)
 
     def near_part(i, carry):
         for head in (2 * i, 2 * i + 1):
@@ -382,29 +360,13 @@
             ext_phi[head, :w, :] = phi_h
             halo_state[head] = dot_tn(phi_h, hv)
             halo_sum[head] = jnp.broadcast_to(jnp.sum(phi_h.astype(F32), 0, keepdims=True), (8, 128))
-            q = head_rows(q_wide, head, rows, heads).astype(BF16)
-            q_heads[head] = q
-            soft = features(q, map_q)
-            soft_q[head] = soft
-            phi_q = soft.astype(BF16)
-            for c in range(2):
-                block, span = pl.ds(c * w, w), pl.ds(c * w, rows)
-                in_window, in_far = masks(c)
-                scores = dot_nt(q[c * w : (c + 1) * w], ext_k[head, span, :]) * scale
-                scores = jnp.where(in_window, scores, -jnp.inf)
-                top = jnp.max(scores, -1, keepdims=True)
-                damping = jnp.exp(-top)
-                far = damping * dot_nt(phi_q[c * w : (c + 1) * w], ext_phi[head, span, :])
-                weight = jnp.exp(scores - top) + jnp.where(in_far, far, 0.0)
-                numer_near[head, block, :] = dot_nn(weight.astype(BF16), ext_v[head, span, :])
-                denom_near[head, block, :] = jnp.sum(weight, -1, keepdims=True)
-                damp[head, block, :] = damping
+            near_block(head, 0, q_heads[head, :w, :], soft_q[head, :w, :].astype(BF16))
 
         @pl.when(i == 4)
         def _():
             forward.collect()
 
-        @pl.when(i == 6)
+        @pl.when(i == 7)
         def _():
             forward.spread()
 
@@ -437,7 +399,7 @@
                 inverse = 1.0 / (denom_near[head, block, :] + damping * state_den)
                 output = numer * inverse
                 at = pl.ds(c * w * heads + head, w, stride=heads)
-                out_wide[at, :] = output
+                out_ref[at, :] = output
                 d_out = (output - t_wide[at, :]) * (2.0 / total_tokens)
                 d_numer = d_out * inverse
                 d_denom = -jnp.sum(d_out * output, -1, keepdims=True) * inverse
@@ -499,7 +461,6 @@
         return carry
 
     lax.fori_loop(0, heads // 2, far_part, 0)
-    out_ref[...] = out_wide[...].astype(BF16)
 
     @pl.when(has_later)
     def _():
@@ -527,7 +488,9 @@
         return carry
 
     lax.fori_loop(0, heads // 2, last_part, 0)
-    packed[...] = jnp.where(left_half(packed.shape), gq[...], -gk[...])
+    for k in range(PLANE):
+        source = gq if k < PLANE // 2 else gk
+        packed[k] = source[k % (PLANE // 2) * 8 : k % (PLANE // 2) * 8 + 8, :]
     final.give()
     final.collect()
     final.spread()
@@ -537,8 +500,8 @@
 
     @pl.when(has_later)
     def _():
-        halo_copy(0, k_ref).wait_send()
-        halo_copy(1, v_ref).wait_send()
+        halo_copy(0, k_in).wait_send()
+        halo_copy(1, v_in).wait_send()
 
     @pl.when(has_prior)
     def _():
@@ -567,28 +530,36 @@
     layer = pltpu.VMEM((layers, ROWS, size), F32)
     grad = pltpu.VMEM((size, size), F32)
     dma = pltpu.SemaphoreType.DMA
-    in_plane, scan_z, sum_z = dma((PLANE,)), dma((layers,)), dma((others,))
-    scan_sems = [in_plane, in_plane, scan_z, scan_z, in_plane, in_plane]
-    pair_q = jnp.concatenate([map_q, -map_q], 1)
-    pair_k = jnp.concatenate([map_k, -map_k], 1)
+    one = dma(())
+    scan_sems = [one, one, one, one, one, dma((PLANE,))]
+    bf16_flat = pltpu.VMEM(flat, BF16)
+    slice_rows = size // PLANE
     vmem = pl.BlockSpec(memory_space=pltpu.VMEM)
-    hybrid, grads = pl.pallas_call(
+    hbm = pl.BlockSpec(memory_space=pl.ANY)
+    output, grads = pl.pallas_call(
         functools.partial(kernel, heads, total_tokens),
-        out_shape=[jax.ShapeDtypeStruct(flat, BF16), jax.ShapeDtypeStruct((size, size), F32)],
-        in_specs=[vmem] * 6,
+        out_shape=[
+            jax.ShapeDtypeStruct(flat, F32),
+            jax.ShapeDtypeStruct((PLANE, slice_rows, size), F32),
+        ],
+        in_specs=[hbm] * 4 + [vmem] * 2,
         out_specs=[vmem] * 2,
         scratch_shapes=[
-            wide, wide, wide, wide, wide, pltpu.VMEM((2,) + half, BF16), pltpu.VMEM(half, F32), pltpu.VMEM(half, F32),
+            bf16_flat, bf16_flat, bf16_flat, bf16_flat, wide, wide, wide, wide,
+            pltpu.VMEM((2,) + half, BF16), pltpu.VMEM(half, F32), pltpu.VMEM(half, F32),
             ext, ext, ext, pltpu.VMEM((heads, rows, size), BF16), tiles, tiles, tiles, column, column, square, row,
             tiles, column, square, row, tiles, halves, halves,
-            slices, slices, layer, slices, slices, slices, layer, slices, grad, grad, grad,
-            pltpu.VMEM((PLANE, size // PLANE, size), F32), pltpu.VMEM((others, size // PLANE, size), F32),
-            dma((2,)), dma((2,)), dma((heads // 2,)), dma((heads // 2,)),
-            *scan_sems, *scan_sems, in_plane, in_plane, sum_z, sum_z, in_plane, in_plane,
+            slices, slices, layer, slices, slices, slices, layer, slices, grad, grad,
+            pltpu.VMEM((PLANE, slice_rows, size), F32), pltpu.VMEM((PLANE, slice_rows, size), F32),
+            pltpu.VMEM((others, slice_rows, size), F32),
+            dma((4,)), dma((2,)), dma((2,)), dma((heads // 2,)), dma((heads // 2,)),
+            *scan_sems, *scan_sems, one, one, one, one, one, one,
         ],
         compiler_params=pltpu.CompilerParams(vmem_limit_bytes=VMEM_LIMIT, collective_id=0, has_side_effects=True),
-    )(queries.reshape(flat), keys.reshape(flat), values.reshape(flat), target.reshape(flat), pair_q, pair_k)
-    return hybrid.reshape(rows, heads, size), grads[:, :FEAT], grads[:, FEAT:]
+    )(queries.reshape(flat), keys.reshape(flat), values.reshape(flat), target.reshape(flat), map_q.T, map_k.T)
+    hybrid = output.astype(BF16).reshape(rows, heads, size)
+    grads = grads.reshape(size, size)
+    return hybrid, grads[:FEAT].T, grads[FEAT:].T
 
 
 def solution(mesh):

time: 132 us -> 121 us (0.917)
  local copies, waits for them, and re-layouts: 5.92 us -> 0.63 us
  Pallas kernels: 123 us -> 118 us
    pallas_call x1, Pallas kernels: 123 us -> 118 us  [per_device(): pl.pallas_call(functools.partial(kernel, heads, total_tokens), out_shape=...]
    unnamed x9 -> x2, local copies, waits for them, and re-layouts: 4.7 us -> 0.01 us
    convert_element_type x0 -> x1, other arithmetic: none -> 2.1 us  [per_device(): hybrid = output.astype(BF16).reshape(rows, heads, size)]
where the time goes in v3:
time: 121 us
  Pallas kernels  118 us (98%)
  other arithmetic  2.1 us (2%)
    pallas_call x1, Pallas kernels, per_device(): pl.pallas_call(functools.partial(kernel, heads, total_tokens), out_shape=...  118 us

profile of v3, /device:TPU:1, one launch (start us, length us, event | category | flops | bytes accessed | tf_op | source)
XLA Modules:
  0.0 121.0 jit_solution(14578521985872302046)
XLA Ops:
  0.6 117.6 %shard_map.85 = (f32[2048,128]{1,0:T(8,128)}, f32[16,8,128]{2,1,0:T(8,128)}) custom-call(bf16[2048,128]{1,0:T(8,128)(2,1)} %bitcast.16, bf16[2048,128]{1,0:T(8,128)(2,1)} %bitcast.17, bf16[2048,128]{1,0:T(8,128)(2,1)} %bitcast.18, bf16[2048,128]{1,0:T(8,128)(2,1)} %bitcast.19, bf16[64,128]{1,0:T(8,128)(2,1)} %bitcast.20, bf16[64,128]{1,0:T(8,128)(2,1)} %bitcast.21), custom_call_target="tpu_custom_call" | custom-call | tf_op jit(solution)/shard_map/pallas_call | solution.py:539
  118.2 0.0 copy-start
  118.2 2.1 %convert_element_type.3 = bf16[2048,128]{1,0:T(8,128)(2,1)} convert(f32[2048,128]{1,0:T(8,128)} %get-tuple-element.5) | non-fusion elementwise | flops 262144 | bytes 1572864 | tf_op jit(solution)/shard_map/convert_element_type | solution.py:560
  120.3 0.0 copy-done
  120.3 0.6 slice_bitcast_fusion
Async XLA Ops:
  118.2 2.1 %copy-start = (f32[16,8,128]{2,1,0:T(8,128)S(1)}, f32[16,8,128]{2,1,0:T(8,128)}, u32[]{:S(2)}) copy-start(f32[16,8,128]{2,1,0:T(8,128)} %get-tuple-element.6) | copy-start | bytes 196612

commit v4 on v3

v4 whole, which is shorter than its diff:
```python
import functools

import jax
import jax.numpy as jnp
from jax import lax
from jax.experimental import pallas as pl
from jax.experimental.pallas import tpu as pltpu
from jax.sharding import PartitionSpec as P

WINDOW = 64
FEAT = 64
PLANE = 16
ROWS = 136
MESH = pl.DeviceIdType.MESH
F32 = jnp.float32
BF16 = jnp.bfloat16
VMEM_LIMIT = 56 * 1024 * 1024


def dot_nn(a, b):
    return lax.dot_general(a, b, (((1,), (0,)), ((), ())), preferred_element_type=F32)


def dot_nt(a, b):
    return lax.dot_general(a, b, (((1,), (1,)), ((), ())), preferred_element_type=F32)


def dot_tn(a, b):
    return lax.dot_general(a, b, (((0,), (0,)), ((), ())), preferred_element_type=F32)


def split(x):
    high = x.astype(BF16)
    return high, (x - high.astype(F32)).astype(BF16)


def left_half(shape):
    return lax.broadcasted_iota(jnp.int32, shape, len(shape) - 1) < FEAT


def features(x, pair_map):
    hidden = dot_nt(x, pair_map)
    left = left_half(hidden.shape)
    top_left = jnp.max(jnp.where(left, hidden, -jnp.inf), -1, keepdims=True)
    top_right = jnp.max(jnp.where(left, -jnp.inf, hidden), -1, keepdims=True)
    e = jnp.exp(hidden - jnp.where(left, top_left, top_right))
    sum_left = jnp.sum(jnp.where(left, e, 0.0), -1, keepdims=True)
    sum_right = jnp.sum(jnp.where(left, 0.0, e), -1, keepdims=True)
    return e * jnp.where(left, 1.0 / sum_left, 1.0 / sum_right)


def feature_grad(x, soft, upstream):
    left = left_half(soft.shape)
    product = soft * upstream
    inner_left = jnp.sum(jnp.where(left, product, 0.0), -1, keepdims=True)
    inner_right = jnp.sum(jnp.where(left, 0.0, product), -1, keepdims=True)
    part = soft * (upstream - jnp.where(left, inner_left, inner_right))
    u = part - pltpu.roll(part, FEAT, 1)
    return dot_tn(u.astype(BF16), x)


def head_rows(ref, head, rows, heads):
    return ref[pl.ds(head, rows, stride=heads), :]


def widen(src, dst):
    dst[...] = src[...].astype(F32)


def wrapped(k, count):
    return jnp.where(k >= count, k - count, k)


def await_bytes(ref, sem):
    pltpu.make_async_copy(ref, ref, sem).wait()


class Across:
    def __init__(self, totals, send, recv, reverse):
        self.totals, self.send, self.recv, self.reverse = totals, send, recv, reverse
        me = lax.axis_index("seq")
        self.layers = lax.axis_size("seq") // PLANE
        self.z, self.p = me // PLANE, me % PLANE

    def give(self, total):
        self.totals[self.z] = total
        for i in range(1, self.layers):
            other = wrapped(self.z + i, self.layers)
            pltpu.make_async_remote_copy(
                src_ref=self.totals.at[self.z], dst_ref=self.totals.at[self.z], send_sem=self.send, recv_sem=self.recv,
                device_id={"seq": other * PLANE + self.p}, device_id_type=MESH,
            ).start()

    def base(self):
        await_bytes(self.totals.at[pl.ds(0, self.layers - 1)], self.recv)
        base = jnp.zeros(self.totals.shape[1:], F32)
        for k in range(self.layers):
            reached = k > self.z if self.reverse else k < self.z
            base = base + jnp.where(reached, self.totals[k], 0.0)
        return base

    def finish(self):
        await_bytes(self.totals.at[pl.ds(0, self.layers - 1)], self.send)


class Total:
    def __init__(self, x, out, parts, totals, sems):
        self.x, self.out, self.parts, self.totals = x, out, parts, totals
        self.send1, self.recv1, self.send_z, self.recv_z, self.send2, self.recv2 = sems
        me, core = lax.axis_index("seq"), lax.axis_index("head")
        self.cores = lax.axis_size("head")
        self.others = lax.axis_size("seq") // PLANE * self.cores
        self.z, self.p = me // PLANE, me % PLANE
        self.here = self.z * self.cores + core

    def in_plane(self, k):
        return {"seq": self.z * PLANE + k}

    def give(self):
        for i in range(1, PLANE):
            to = wrapped(self.p + i, PLANE)
            pltpu.make_async_remote_copy(
                src_ref=self.x.at[to], dst_ref=self.parts.at[self.p], send_sem=self.send1, recv_sem=self.recv1,
                device_id=self.in_plane(to), device_id_type=MESH,
            ).start()
        pltpu.make_async_copy(self.x.at[self.p], self.parts.at[self.p], self.recv1).start()

    def collect(self):
        await_bytes(self.parts, self.recv1)
        self.totals[self.here] = jnp.sum(self.parts[...], 0)
        for i in range(1, self.others):
            at = wrapped(self.here + i, self.others)
            pltpu.make_async_remote_copy(
                src_ref=self.totals.at[self.here], dst_ref=self.totals.at[self.here],
                send_sem=self.send_z, recv_sem=self.recv_z,
                device_id={"seq": (at // self.cores) * PLANE + self.p, "head": at % self.cores}, device_id_type=MESH,
            ).start()

    def spread(self):
        await_bytes(self.totals.at[pl.ds(0, self.others - 1)], self.recv_z)
        self.out[self.p] = jnp.sum(self.totals[...], 0)
        for i in range(1, PLANE):
            pltpu.make_async_remote_copy(
                src_ref=self.out.at[self.p], dst_ref=self.out.at[self.p], send_sem=self.send2, recv_sem=self.recv2,
                device_id=self.in_plane(wrapped(self.p + i, PLANE)), device_id_type=MESH,
            ).start()

    def finish(self):
        most = pl.ds(0, PLANE - 1)
        await_bytes(self.out.at[most], self.recv2)
        await_bytes(self.out.at[most], self.send2)
        await_bytes(self.x.at[most], self.send1)
        await_bytes(self.totals.at[pl.ds(0, self.others - 1)], self.send_z)


def greet():
    me, core = lax.axis_index("seq"), lax.axis_index("head")
    count, cores = lax.axis_size("seq"), lax.axis_size("head")
    others = count // PLANE * cores
    z, p = me // PLANE, me % PLANE
    barrier = pltpu.get_barrier_semaphore()

    def plane(i, carry):
        device = {"seq": z * PLANE + (p + i) % PLANE}
        pl.semaphore_signal(barrier, inc=1, device_id=device, device_id_type=MESH)
        return carry

    def beyond(i, carry):
        at = (z * cores + core + i) % others
        device = {"seq": (at // cores) * PLANE + p, "head": at % cores}
        pl.semaphore_signal(barrier, inc=1, device_id=device, device_id_type=MESH)
        return carry

    lax.fori_loop(1, PLANE, plane, 0)
    lax.fori_loop(1, others, beyond, 0)
    return PLANE - 1 + others - 1


def kernel(
    heads, total_tokens, q_ref, k_ref, v_ref, t_ref, mq_ref, mk_ref, out_ref, grad_ref,
    k_in, v_in, q_in, t_in, k_wide, v_wide, q_wide, t_wide, mine, held,
    phi_all, soft_q, soft_k, numer_near, denom_near, damp, state, halo_state, d_numer_all, d_denom_all,
    gstate, near, lead, total, totals1, totals2, out_send, out_held, gq, gk, packed, parts3, totals3,
    load, send, recv, send_halo, recv_halo, send_lead, recv_lead, send_out, recv_out, *sems,
):
    w = WINDOW
    rows = 2 * w
    chunks = PLANE
    K, V, Q, T = range(4)
    greeted = greet()
    arrays = [(k_ref, k_in, k_wide), (v_ref, v_in, v_wide), (q_ref, q_in, q_wide), (t_ref, t_in, t_wide)]
    loads = [pltpu.make_async_copy(source, into, load.at[i]) for i, (source, into, wide) in enumerate(arrays)]
    for copy in loads:
        copy.start()
    me = lax.axis_index("seq")
    layers = lax.axis_size("seq") // PLANE
    z, p = me // PLANE, me % PLANE
    has_prior = z > 0
    has_later = z < layers - 1
    forward = Across(totals1, sems[0], sems[1], False)
    backward = Across(totals2, sems[2], sems[3], True)
    final = Total(packed, grad_ref, parts3, totals3, sems[4:10])

    def in_plane(k):
        return {"seq": z * PLANE + k}

    halo_there = held.at[0, pl.ds(0, 2), pl.ds(w, w)]
    halo_copy = pltpu.make_async_remote_copy(
        src_ref=held.at[chunks, pl.ds(0, 2), pl.ds(w, w)], dst_ref=halo_there, send_sem=send_halo, recv_sem=recv_halo,
        device_id={"seq": jnp.where(has_later, z + 1, 0) * PLANE + p}, device_id_type=MESH,
    )
    lead_copy = pltpu.make_async_remote_copy(
        src_ref=lead.at[0], dst_ref=lead.at[chunks], send_sem=send_lead, recv_sem=recv_lead,
        device_id={"seq": jnp.where(has_prior, z - 1, layers - 1) * PLANE + p}, device_id_type=MESH,
    )

    for copy, (source, into, wide) in zip(loads, arrays):
        copy.wait()
        widen(into, wide)
    pl.semaphore_wait(pltpu.get_barrier_semaphore(), greeted)

    def give(i, carry):
        head = wrapped(p + i, PLANE)
        for j, (source, into, wide) in enumerate(arrays):
            mine[head, j] = head_rows(wide, head, rows, heads).astype(BF16)

        @pl.when(i > 0)
        def _():
            pltpu.make_async_remote_copy(
                src_ref=mine.at[head], dst_ref=held.at[p + 1], send_sem=send, recv_sem=recv.at[p],
                device_id=in_plane(head), device_id_type=MESH,
            ).start()

        @pl.when(i == 0)
        def _():
            pltpu.make_async_copy(mine.at[head], held.at[p + 1], recv.at[p]).start()

        return carry

    lax.fori_loop(0, heads, give, 0)

    map_q, map_k = (
        jnp.concatenate([ref[...], (-ref[...].astype(F32)).astype(BF16)], 0) for ref in (mq_ref, mk_ref)
    )
    row = lax.broadcasted_iota(jnp.int32, (w, rows), 0)
    col = lax.broadcasted_iota(jnp.int32, (w, rows), 1)
    scale = 128 ** (-0.5)
    total[...] = jnp.zeros_like(total)

    def masks(first):
        in_window = (col > row) & (col <= row + w)
        in_far = col <= row
        if not first:
            return in_window, in_far
        live = (col >= w) | has_prior
        return in_window & live, in_far & live

    def before(c):
        return jnp.where(c == 0, 1, c)

    def ext(ref, slot, c):
        return jnp.concatenate([ref[slot, w:, :], ref[c + 1, :w, :]], 0)

    def near_block(c, half, kn, vn, pn, first):
        block = pl.ds(half * w, w)
        in_window, in_far = masks(first)
        scores = jnp.where(in_window, dot_nt(held[c + 1, Q, block, :], kn) * scale, -jnp.inf)
        top = jnp.max(scores, -1, keepdims=True)
        damping = jnp.exp(-top)
        far = damping * dot_nt(soft_q[c, block, :].astype(BF16), pn)
        weight = jnp.exp(scores - top) + jnp.where(in_far, far, 0.0)
        numer_near[c, block, :] = dot_nn(weight.astype(BF16), vn)
        denom_near[c, block, :] = jnp.sum(weight, -1, keepdims=True)
        damp[c, block, :] = damping

    def first_block(c, slot, first=False):
        near_block(c, 0, ext(held.at[:, K], slot, c), ext(held.at[:, V], slot, c), ext(phi_all, slot, c), first)

    def own_part(i, carry):
        c1 = wrapped(p + PLANE - 2 * i, PLANE)
        c2 = wrapped(p + PLANE - 2 * i - 1, PLANE)
        for c in (c1, c2):
            await_bytes(held.at[c + 1], recv.at[c])

            @pl.when((c == chunks - 1) & has_later)
            def _():
                halo_copy.start()

        for c in (c1, c2):
            soft = features(held[c + 1, K], map_k)
            soft_k[c] = soft
            phi = soft.astype(BF16)
            phi_all[c + 1] = phi
            v = held[c + 1, V]
            for half in range(2):
                part = phi[half * w : (half + 1) * w]
                block_state = dot_tn(part, v[half * w : (half + 1) * w])
                block_sum = jnp.sum(part.astype(F32), 0, keepdims=True)
                state[2 * c + half, :128, :] = block_state
                state[2 * c + half, 128:, :] = jnp.broadcast_to(block_sum, (ROWS - 128, 128))
                total[:128, :] += block_state
                total[128:, :] += block_sum
            soft_q[c] = features(held[c + 1, Q], map_q)
            near_block(c, 1, held[c + 1, K], v, phi, False)
        first_block(c1, before(c1))

        @pl.when(i > 0)
        def _():
            c = wrapped(c1 + 1, PLANE)
            first_block(c, before(c))

        return carry

    lax.fori_loop(0, chunks // 2, own_part, 0)
    forward.give(total[...])
    final_chunk = wrapped(p + 1, PLANE)
    first_block(final_chunk, before(final_chunk))

    @pl.when(has_prior)
    def _():
        await_bytes(halo_there, recv_halo)

    @pl.when(jnp.logical_not(has_prior))
    def _():
        held[0, :2, w:, :] = jnp.zeros((2, w, 128), BF16)

    phi_halo = jnp.where(has_prior, features(held[0, K, w:, :], map_k), 0.0).astype(BF16)
    phi_all[0, w:, :] = phi_halo
    halo_state[:128, :] = dot_tn(phi_halo, held[0, V, w:, :])
    halo_state[128:, :] = jnp.broadcast_to(jnp.sum(phi_halo.astype(F32), 0, keepdims=True), (ROWS - 128, 128))
    first_block(0, 0, True)

    base = forward.base()

    def lead_states(b, carry):
        now, after = carry
        own = state[b]
        state[b] = now
        return after, after + own

    lax.fori_loop(0, 2 * chunks, lead_states, (base - halo_state[...], base))
    total[...] = jnp.zeros_like(total)

    def middle_part(i, carry):
        pair = (2 * i, 2 * i + 1)
        for c in pair:
            phi_q = soft_q[c].astype(BF16)
            target = held[c + 1, T].astype(F32)
            for half in range(2):
                block, span, b = pl.ds(half * w, w), slice(half * w, (half + 1) * w), 2 * c + half
                pq = phi_q[span]
                wide_pq = pq.astype(F32)
                damping = damp[c, block, :]
                high, low = split(state[b, :128, :])
                state_den = jnp.sum(wide_pq * state[b, 128:129, :], -1, keepdims=True)
                numer = numer_near[c, block, :] + damping * (dot_nn(pq, high) + dot_nn(pq, low))
                inverse = 1.0 / (denom_near[c, block, :] + damping * state_den)
                output = numer * inverse
                out_send[c, block, :] = output.astype(BF16)
                d_out = (output - target[span]) * (2.0 / total_tokens)
                d_numer = d_out * inverse
                d_denom = -jnp.sum(d_out * output, -1, keepdims=True) * inverse
                d_numer_all[c, block, :] = d_numer
                d_denom_all[c, block, :] = d_denom
                g_state = dot_tn(pq, (damping * d_numer).astype(BF16))
                g_sum = jnp.sum(damping * d_denom * wide_pq, 0, keepdims=True)
                gstate[b, :128, :] = g_state
                gstate[b, 128:, :] = jnp.broadcast_to(g_sum, (ROWS - 128, 128))
                total[:128, :] += g_state
                total[128:, :] += g_sum
        return carry

    lax.fori_loop(0, chunks // 2, middle_part, 0)
    backward.give(total[...])

    def give_out(i, carry):
        c = wrapped(p + i, PLANE)
        pltpu.make_async_remote_copy(
            src_ref=out_send.at[c], dst_ref=out_held.at[p], send_sem=send_out, recv_sem=recv_out,
            device_id=in_plane(c), device_id_type=MESH,
        ).start()
        return carry

    lax.fori_loop(1, PLANE, give_out, 0)
    pltpu.make_async_copy(out_send.at[p], out_held.at[p], recv_out).start()
    gq[...] = jnp.zeros_like(gq)
    gk[...] = jnp.zeros_like(gk)

    def far_part(i, carry):
        for c in (2 * i, 2 * i + 1):
            soft = soft_q[c]
            phi_q = soft.astype(BF16)
            d_phi, d_near = [], []
            for half in range(2):
                block, b = pl.ds(half * w, w), 2 * c + half
                if half:
                    in_far = masks(False)[1]
                    vn, pn = held[c + 1, V], phi_all[c + 1]
                else:
                    in_far = (col <= row) & ((col >= w) | has_prior | (c > 0))
                    vn, pn = ext(held.at[:, V], c, c), ext(phi_all, c, c)
                damping = damp[c, block, :]
                d_numer = d_numer_all[c, block, :]
                d_denom = d_denom_all[c, block, :]
                high, low = split(state[b, :128, :])
                dn_high, dn_low = split(d_numer)
                far_grad = damping * (dot_nt(dn_high, vn) + d_denom)
                far_grad = jnp.where(in_far, far_grad, 0.0).astype(BF16)
                through = dot_nt(dn_high, high) + dot_nt(dn_high, low) + dot_nt(dn_low, high)
                d_phi.append(dot_nn(far_grad, pn) + damping * (through + d_denom * state[b, 128:129, :]))
                d_near.append(dot_tn(far_grad, phi_q[half * w : (half + 1) * w]))
            lead[c] = d_near[0][:w]
            near[c, :w, :] = d_near[0][w:] + d_near[1][:w]
            near[c, w:, :] = d_near[1][w:]
            gq[...] += feature_grad(held[c + 1, Q], soft, jnp.concatenate(d_phi, 0))

        @pl.when((i == 0) & has_prior)
        def _():
            high, low = split(gstate[0, :128, :])
            hv = held[0, V, w:, :]
            lead[0] = lead[0] - (dot_nt(hv, high) + dot_nt(hv, low) + gstate[0, 128:129, :])
            lead_copy.start()

        return carry

    lax.fori_loop(0, chunks // 2, far_part, 0)

    base = backward.base()

    def tail_states(i, carry):
        now, after = carry
        b = 2 * chunks - 1 - i
        own = gstate[b]
        gstate[b] = now
        return after, after + own

    lax.fori_loop(0, 2 * chunks, tail_states, (base, base))

    @pl.when(has_later)
    def _():
        await_bytes(lead.at[chunks], recv_lead)

    @pl.when(jnp.logical_not(has_later))
    def _():
        lead[chunks] = jnp.zeros(lead.shape[1:], F32)

    def last_part(i, carry):
        for c in (2 * i, 2 * i + 1):
            d_phi = []
            for half in range(2):
                v, b = held[c + 1, V, half * w : (half + 1) * w, :], 2 * c + half
                high, low = split(gstate[b, :128, :])
                d_phi.append(dot_nt(v, high) + dot_nt(v, low) + gstate[b, 128:129, :])
            d_phi = [d_phi[0] + near[c, :w, :], d_phi[1] + (near[c, w:, :] + lead[c + 1])]
            gk[...] += feature_grad(held[c + 1, K], soft_k[c], jnp.concatenate(d_phi, 0))
        return carry

    lax.fori_loop(0, chunks // 2, last_part, 0)
    for k in range(PLANE):
        source = gq if k < PLANE // 2 else gk
        packed[k] = source[k % (PLANE // 2) * 8 : k % (PLANE // 2) * 8 + 8, :]
    final.give()
    await_bytes(out_held, recv_out)

    def arrange(i, carry):
        for head in (2 * i, 2 * i + 1):
            out_ref[pl.ds(head, rows, stride=heads), :] = out_held[head].astype(F32)
        return carry

    lax.fori_loop(0, heads // 2, arrange, 0)
    final.collect()
    final.spread()
    most = pl.ds(0, PLANE - 1)
    await_bytes(mine.at[most], send)
    await_bytes(out_send.at[most], send_out)
    forward.finish()
    backward.finish()

    @pl.when(has_later)
    def _():
        halo_copy.wait_send()

    @pl.when(has_prior)
    def _():
        lead_copy.wait_send()

    final.finish()


def per_device(queries, keys, values, target, map_q, map_k):
    rows, heads, size = queries.shape
    total_tokens = rows * lax.axis_size("seq")
    layers = lax.axis_size("seq") // PLANE
    others = layers * lax.axis_size("head")
    chunks = PLANE
    flat = (rows * heads, size)
    wide = pltpu.VMEM(flat, F32)
    narrow = pltpu.VMEM(flat, BF16)
    tiles = pltpu.VMEM((chunks, rows, size), F32)
    tiles16 = pltpu.VMEM((chunks, rows, size), BF16)
    column = pltpu.VMEM((chunks, rows, 1), F32)
    states = pltpu.VMEM((2 * chunks, ROWS, size), F32)
    state = pltpu.VMEM((ROWS, size), F32)
    layer = pltpu.VMEM((layers, ROWS, size), F32)
    grad = pltpu.VMEM((size, size), F32)
    slices = pltpu.VMEM((PLANE, size // PLANE, size), F32)
    dma = pltpu.SemaphoreType.DMA
    one = dma(())
    vmem = pl.BlockSpec(memory_space=pltpu.VMEM)
    hbm = pl.BlockSpec(memory_space=pl.ANY)
    output, grads = pl.pallas_call(
        functools.partial(kernel, heads, total_tokens),
        out_shape=[
            jax.ShapeDtypeStruct(flat, F32),
            jax.ShapeDtypeStruct((PLANE, size // PLANE, size), F32),
        ],
        in_specs=[hbm] * 4 + [vmem] * 2,
        out_specs=[vmem] * 2,
        scratch_shapes=[
            narrow, narrow, narrow, narrow, wide, wide, wide, wide,
            pltpu.VMEM((heads, 4, rows, size), BF16), pltpu.VMEM((chunks + 1, 4, rows, size), BF16),
            pltpu.VMEM((chunks + 1, rows, size), BF16), tiles, tiles, tiles, column, column, states, state, tiles, column,
            states, tiles, pltpu.VMEM((chunks + 1, WINDOW, size), F32), state, layer, layer, tiles16, tiles16,
            grad, grad, slices, slices, pltpu.VMEM((others, size // PLANE, size), F32),
            dma((4,)), one, dma((PLANE,)), one, one, one, one, one, one, *[one] * 10,
        ],
        compiler_params=pltpu.CompilerParams(vmem_limit_bytes=VMEM_LIMIT, collective_id=0, has_side_effects=True),
    )(*(array.reshape(flat) for array in (queries, keys, values, target)), map_q.T, map_k.T)
    hybrid = output.astype(BF16).reshape(rows, heads, size)
    grads = grads.reshape(size, size)
    return hybrid, grads[:FEAT].T, grads[FEAT:].T


def solution(mesh):
    tokens = P("seq", "head", None)
    return jax.shard_map(
        per_device,
        mesh=mesh,
        in_specs=(tokens, tokens, tokens, tokens, P(), P()),
        out_specs=(tokens, P(), P()),
        check_vma=False,
    )
```

time: 121 us -> 105 us (0.87)
  Pallas kernels: 118 us -> 101 us
    pallas_call x1, Pallas kernels: 118 us -> 101 us  [per_device(): pl.pallas_call(functools.partial(kernel, heads, total_tokens), out_shape=...]
where the time goes in v4:
time: 105 us
  Pallas kernels  101 us (96%)
  other arithmetic  2.1 us (2%)
    pallas_call x1, Pallas kernels, per_device(): pl.pallas_call(functools.partial(kernel, heads, total_tokens), out_shape=...  101 us
    convert_element_type x1, other arithmetic, per_device(): hybrid = output.astype(BF16).reshape(rows, heads, size)  2.1 us

profile of v4, /device:TPU:1, one launch (start us, length us, event | category | flops | bytes accessed | tf_op | source)
XLA Modules:
  0.0 104.9 jit_solution(15651088781384049268)
XLA Ops:
  0.6 101.5 %shard_map.85 = (f32[2048,128]{1,0:T(8,128)}, f32[16,8,128]{2,1,0:T(8,128)}) custom-call(bf16[2048,128]{1,0:T(8,128)(2,1)} %bitcast.16, bf16[2048,128]{1,0:T(8,128)(2,1)} %bitcast.17, bf16[2048,128]{1,0:T(8,128)(2,1)} %bitcast.18, bf16[2048,128]{1,0:T(8,128)(2,1)} %bitcast.19, bf16[64,128]{1,0:T(8,128)(2,1)} %bitcast.20, bf16[64,128]{1,0:T(8,128)(2,1)} %bitcast.21), custom_call_target="tpu_custom_call" | custom-call | tf_op jit(solution)/shard_map/pallas_call | solution.py:511
  102.1 0.0 copy-start
  102.1 2.1 %convert_element_type.3 = bf16[2048,128]{1,0:T(8,128)(2,1)} convert(f32[2048,128]{1,0:T(8,128)} %get-tuple-element.5) | non-fusion elementwise | flops 262144 | bytes 1572864 | tf_op jit(solution)/shard_map/convert_element_type | solution.py:529
  104.2 0.0 copy-done
  104.2 0.6 slice_bitcast_fusion
Async XLA Ops:
  102.1 2.1 %copy-start = (f32[16,8,128]{2,1,0:T(8,128)S(1)}, f32[16,8,128]{2,1,0:T(8,128)}, u32[]{:S(2)}) copy-start(f32[16,8,128]{2,1,0:T(8,128)} %get-tuple-element.6) | copy-start | bytes 196612

commit v5 on v4

--- a/solution.py
+++ b/solution.py
@@ -180,7 +180,7 @@
     heads, total_tokens, q_ref, k_ref, v_ref, t_ref, mq_ref, mk_ref, out_ref, grad_ref,
     k_in, v_in, q_in, t_in, k_wide, v_wide, q_wide, t_wide, mine, held,
     phi_all, soft_q, soft_k, numer_near, denom_near, damp, state, halo_state, d_numer_all, d_denom_all,
-    gstate, near, lead, total, totals1, totals2, out_send, out_held, gq, gk, packed, parts3, totals3,
+    gstate, state16, state_sum, later16, later_sum, near, lead, total, totals1, totals2, out_send, out_held, gq, gk, packed, parts3, totals3,
     load, send, recv, send_halo, recv_halo, send_lead, recv_lead, send_out, recv_out, *sems,
 ):
     w = WINDOW
@@ -214,30 +214,39 @@
         device_id={"seq": jnp.where(has_prior, z - 1, layers - 1) * PLANE + p}, device_id_type=MESH,
     )
 
-    for copy, (source, into, wide) in zip(loads, arrays):
-        copy.wait()
-        widen(into, wide)
-    pl.semaphore_wait(pltpu.get_barrier_semaphore(), greeted)
-
-    def give(i, carry):
-        head = wrapped(p + i, PLANE)
-        for j, (source, into, wide) in enumerate(arrays):
-            mine[head, j] = head_rows(wide, head, rows, heads).astype(BF16)
-
-        @pl.when(i > 0)
-        def _():
-            pltpu.make_async_remote_copy(
-                src_ref=mine.at[head], dst_ref=held.at[p + 1], send_sem=send, recv_sem=recv.at[p],
-                device_id=in_plane(head), device_id_type=MESH,
-            ).start()
-
-        @pl.when(i == 0)
-        def _():
-            pltpu.make_async_copy(mine.at[head], held.at[p + 1], recv.at[p]).start()
-
-        return carry
-
-    lax.fori_loop(0, heads, give, 0)
+    def give(wave, first):
+        def step(i, carry):
+            for head in (wrapped(p + 2 * i, PLANE), wrapped(p + 2 * i + 1, PLANE)):
+                for j in wave:
+                    mine[head, j] = head_rows(arrays[j][2], head, rows, heads).astype(BF16)
+            part = pl.ds(wave[0], len(wave))
+            for k in range(2):
+                head = wrapped(p + 2 * i + k, PLANE)
+
+                @pl.when(head != p)
+                def _():
+                    pltpu.make_async_remote_copy(
+                        src_ref=mine.at[head, part], dst_ref=held.at[p + 1, part],
+                        send_sem=send, recv_sem=recv.at[first + p],
+                        device_id=in_plane(head), device_id_type=MESH,
+                    ).start()
+
+                @pl.when(head == p)
+                def _():
+                    pltpu.make_async_copy(mine.at[head, part], held.at[p + 1, part], recv.at[first + p]).start()
+
+            return carry
+
+        for j in wave:
+            loads[j].wait()
+            widen(arrays[j][1], arrays[j][2])
+        if first == 0:
+            pl.semaphore_wait(pltpu.get_barrier_semaphore(), greeted)
+        lax.fori_loop(0, heads // 2, step, 0)
+
+    give((K, V), 0)
+    give((Q,), PLANE)
+    give((T,), 2 * PLANE)
 
     map_q, map_k = (
         jnp.concatenate([ref[...], (-ref[...].astype(F32)).astype(BF16)], 0) for ref in (mq_ref, mk_ref)
@@ -247,46 +256,30 @@
     scale = 128 ** (-0.5)
     total[...] = jnp.zeros_like(total)
 
-    def masks(first):
+    def masks(c, half):
         in_window = (col > row) & (col <= row + w)
         in_far = col <= row
-        if not first:
+        if half:
             return in_window, in_far
-        live = (col >= w) | has_prior
+        live = (col >= w) | has_prior | (c > 0)
         return in_window & live, in_far & live
 
-    def before(c):
-        return jnp.where(c == 0, 1, c)
-
-    def ext(ref, slot, c):
-        return jnp.concatenate([ref[slot, w:, :], ref[c + 1, :w, :]], 0)
-
-    def near_block(c, half, kn, vn, pn, first):
-        block = pl.ds(half * w, w)
-        in_window, in_far = masks(first)
-        scores = jnp.where(in_window, dot_nt(held[c + 1, Q, block, :], kn) * scale, -jnp.inf)
-        top = jnp.max(scores, -1, keepdims=True)
-        damping = jnp.exp(-top)
-        far = damping * dot_nt(soft_q[c, block, :].astype(BF16), pn)
-        weight = jnp.exp(scores - top) + jnp.where(in_far, far, 0.0)
-        numer_near[c, block, :] = dot_nn(weight.astype(BF16), vn)
-        denom_near[c, block, :] = jnp.sum(weight, -1, keepdims=True)
-        damp[c, block, :] = damping
-
-    def first_block(c, slot, first=False):
-        near_block(c, 0, ext(held.at[:, K], slot, c), ext(held.at[:, V], slot, c), ext(phi_all, slot, c), first)
-
-    def own_part(i, carry):
-        c1 = wrapped(p + PLANE - 2 * i, PLANE)
-        c2 = wrapped(p + PLANE - 2 * i - 1, PLANE)
-        for c in (c1, c2):
-            await_bytes(held.at[c + 1], recv.at[c])
+    def ext(ref, c):
+        return jnp.concatenate([ref[c, w:, :], ref[c + 1, :w, :]], 0)
+
+    def arriving(i):
+        return wrapped(p + PLANE - 2 * i, PLANE), wrapped(p + PLANE - 2 * i - 1, PLANE)
+
+    def key_part(i, carry):
+        pair = arriving(i)
+        for c in pair:
+            await_bytes(held.at[c + 1, pl.ds(K, 2)], recv.at[c])
 
             @pl.when((c == chunks - 1) & has_later)
             def _():
                 halo_copy.start()
 
-        for c in (c1, c2):
+        for c in pair:
             soft = features(held[c + 1, K], map_k)
             soft_k[c] = soft
             phi = soft.astype(BF16)
@@ -300,21 +293,10 @@
                 state[2 * c + half, 128:, :] = jnp.broadcast_to(block_sum, (ROWS - 128, 128))
                 total[:128, :] += block_state
                 total[128:, :] += block_sum
-            soft_q[c] = features(held[c + 1, Q], map_q)
-            near_block(c, 1, held[c + 1, K], v, phi, False)
-        first_block(c1, before(c1))
-
-        @pl.when(i > 0)
-        def _():
-            c = wrapped(c1 + 1, PLANE)
-            first_block(c, before(c))
-
-        return carry
-
-    lax.fori_loop(0, chunks // 2, own_part, 0)
+        return carry
+
+    lax.fori_loop(0, chunks // 2, key_part, 0)
     forward.give(total[...])
-    final_chunk = wrapped(p + 1, PLANE)
-    first_block(final_chunk, before(final_chunk))
 
     @pl.when(has_prior)
     def _():
@@ -328,21 +310,55 @@
     phi_all[0, w:, :] = phi_halo
     halo_state[:128, :] = dot_tn(phi_halo, held[0, V, w:, :])
     halo_state[128:, :] = jnp.broadcast_to(jnp.sum(phi_halo.astype(F32), 0, keepdims=True), (ROWS - 128, 128))
-    first_block(0, 0, True)
+
+    def near_part(i, carry):
+        pair = arriving(i)
+        for c in pair:
+            await_bytes(held.at[c + 1, pl.ds(Q, 1)], recv.at[PLANE + c])
+        for c in pair:
+            soft = features(held[c + 1, Q], map_q)
+            soft_q[c] = soft
+            phi_q = soft.astype(BF16)
+            for half in range(2):
+                block, span = pl.ds(half * w, w), slice(half * w, (half + 1) * w)
+                if half:
+                    kn, vn, pn = held[c + 1, K], held[c + 1, V], phi_all[c + 1]
+                else:
+                    kn, vn, pn = ext(held.at[:, K], c), ext(held.at[:, V], c), ext(phi_all, c)
+                in_window, in_far = masks(c, half)
+                scores = jnp.where(in_window, dot_nt(held[c + 1, Q, span, :], kn) * scale, -jnp.inf)
+                top = jnp.max(scores, -1, keepdims=True)
+                damping = jnp.exp(-top)
+                far = damping * dot_nt(phi_q[span], pn)
+                weight = jnp.exp(scores - top) + jnp.where(in_far, far, 0.0)
+                numer_near[c, block, :] = dot_nn(weight.astype(BF16), vn)
+                denom_near[c, block, :] = jnp.sum(weight, -1, keepdims=True)
+                damp[c, block, :] = damping
+        return carry
+
+    lax.fori_loop(0, chunks // 2, near_part, 0)
+
+    def store_split(into, sums, b, whole):
+        high, low = split(whole[:128])
+        into[b, :128, :] = high
+        into[b, 128:, :] = low
+        sums[b] = whole[128:]
 
     base = forward.base()
 
     def lead_states(b, carry):
         now, after = carry
         own = state[b]
-        state[b] = now
+        store_split(state16, state_sum, b, now)
         return after, after + own
 
     lax.fori_loop(0, 2 * chunks, lead_states, (base - halo_state[...], base))
     total[...] = jnp.zeros_like(total)
 
     def middle_part(i, carry):
-        pair = (2 * i, 2 * i + 1)
+        pair = arriving(i)
+        for c in pair:
+            await_bytes(held.at[c + 1, pl.ds(T, 1)], recv.at[2 * PLANE + c])
         for c in pair:
             phi_q = soft_q[c].astype(BF16)
             target = held[c + 1, T].astype(F32)
@@ -351,9 +367,9 @@
                 pq = phi_q[span]
                 wide_pq = pq.astype(F32)
                 damping = damp[c, block, :]
-                high, low = split(state[b, :128, :])
-                state_den = jnp.sum(wide_pq * state[b, 128:129, :], -1, keepdims=True)
-                numer = numer_near[c, block, :] + damping * (dot_nn(pq, high) + dot_nn(pq, low))
+                state_den = jnp.sum(wide_pq * state_sum[b, 0:1, :], -1, keepdims=True)
+                state_num = dot_nn(jnp.concatenate([pq, pq], 1), state16[b])
+                numer = numer_near[c, block, :] + damping * state_num
                 inverse = 1.0 / (denom_near[c, block, :] + damping * state_den)
                 output = numer * inverse
                 out_send[c, block, :] = output.astype(BF16)
@@ -387,32 +403,33 @@
     gk[...] = jnp.zeros_like(gk)
 
     def far_part(i, carry):
+        d_phi = []
+        pair = pl.ds(2 * i, 2)
         for c in (2 * i, 2 * i + 1):
-            soft = soft_q[c]
-            phi_q = soft.astype(BF16)
-            d_phi, d_near = [], []
+            phi_q = soft_q[c].astype(BF16)
+            d_near = []
             for half in range(2):
                 block, b = pl.ds(half * w, w), 2 * c + half
+                in_far = masks(c, half)[1]
                 if half:
-                    in_far = masks(False)[1]
                     vn, pn = held[c + 1, V], phi_all[c + 1]
                 else:
-                    in_far = (col <= row) & ((col >= w) | has_prior | (c > 0))
-                    vn, pn = ext(held.at[:, V], c, c), ext(phi_all, c, c)
+                    vn, pn = ext(held.at[:, V], c), ext(phi_all, c)
                 damping = damp[c, block, :]
                 d_numer = d_numer_all[c, block, :]
                 d_denom = d_denom_all[c, block, :]
-                high, low = split(state[b, :128, :])
-                dn_high, dn_low = split(d_numer)
-                far_grad = damping * (dot_nt(dn_high, vn) + d_denom)
+                high, low = split(damping * d_numer)
+                far_grad = damping * (dot_nt(d_numer.astype(BF16), vn) + d_denom)
                 far_grad = jnp.where(in_far, far_grad, 0.0).astype(BF16)
-                through = dot_nt(dn_high, high) + dot_nt(dn_high, low) + dot_nt(dn_low, high)
-                d_phi.append(dot_nn(far_grad, pn) + damping * (through + d_denom * state[b, 128:129, :]))
+                through = dot_nt(high, state16[b])
+                through = through[:, :128] + through[:, 128:] + dot_nt(low, state16[b, :128, :])
+                d_phi.append(dot_nn(far_grad, pn) + through + damping * d_denom * state_sum[b, 0:1, :])
                 d_near.append(dot_tn(far_grad, phi_q[half * w : (half + 1) * w]))
             lead[c] = d_near[0][:w]
             near[c, :w, :] = d_near[0][w:] + d_near[1][:w]
             near[c, w:, :] = d_near[1][w:]
-            gq[...] += feature_grad(held[c + 1, Q], soft, jnp.concatenate(d_phi, 0))
+        x = jnp.concatenate([held[2 * i + 1, Q], held[2 * i + 2, Q]], 0)
+        gq[...] += feature_grad(x, soft_q[pair].reshape(2 * rows, 128), jnp.concatenate(d_phi, 0))
 
         @pl.when((i == 0) & has_prior)
         def _():
@@ -431,7 +448,7 @@
         now, after = carry
         b = 2 * chunks - 1 - i
         own = gstate[b]
-        gstate[b] = now
+        store_split(later16, later_sum, b, now)
         return after, after + own
 
     lax.fori_loop(0, 2 * chunks, tail_states, (base, base))
@@ -445,14 +462,17 @@
         lead[chunks] = jnp.zeros(lead.shape[1:], F32)
 
     def last_part(i, carry):
+        d_phi = []
+        pair = pl.ds(2 * i, 2)
         for c in (2 * i, 2 * i + 1):
-            d_phi = []
             for half in range(2):
-                v, b = held[c + 1, V, half * w : (half + 1) * w, :], 2 * c + half
-                high, low = split(gstate[b, :128, :])
-                d_phi.append(dot_nt(v, high) + dot_nt(v, low) + gstate[b, 128:129, :])
-            d_phi = [d_phi[0] + near[c, :w, :], d_phi[1] + (near[c, w:, :] + lead[c + 1])]
-            gk[...] += feature_grad(held[c + 1, K], soft_k[c], jnp.concatenate(d_phi, 0))
+                span, b = slice(half * w, (half + 1) * w), 2 * c + half
+                far = dot_nt(held[c + 1, V, span, :], later16[b])
+                far = far[:, :128] + far[:, 128:] + later_sum[b, 0:1, :]
+                d_near = near[c, span, :]
+                d_phi.append(far + (d_near + lead[c + 1] if half else d_near))
+        x = jnp.concatenate([held[2 * i + 1, K], held[2 * i + 2, K]], 0)
+        gk[...] += feature_grad(x, soft_k[pair].reshape(2 * rows, 128), jnp.concatenate(d_phi, 0))
         return carry
 
     lax.fori_loop(0, chunks // 2, last_part, 0)
@@ -501,6 +521,8 @@
     column = pltpu.VMEM((chunks, rows, 1), F32)
     states = pltpu.VMEM((2 * chunks, ROWS, size), F32)
     state = pltpu.VMEM((ROWS, size), F32)
+    split_states = pltpu.VMEM((2 * chunks, 2 * size, size), BF16)
+    state_sums = pltpu.VMEM((2 * chunks, ROWS - 128, size), F32)
     layer = pltpu.VMEM((layers, ROWS, size), F32)
     grad = pltpu.VMEM((size, size), F32)
     slices = pltpu.VMEM((PLANE, size // PLANE, size), F32)
@@ -520,9 +542,10 @@
             narrow, narrow, narrow, narrow, wide, wide, wide, wide,
             pltpu.VMEM((heads, 4, rows, size), BF16), pltpu.VMEM((chunks + 1, 4, rows, size), BF16),
             pltpu.VMEM((chunks + 1, rows, size), BF16), tiles, tiles, tiles, column, column, states, state, tiles, column,
-            states, tiles, pltpu.VMEM((chunks + 1, WINDOW, size), F32), state, layer, layer, tiles16, tiles16,
+            states, split_states, state_sums, split_states, state_sums, tiles,
+            pltpu.VMEM((chunks + 1, WINDOW, size), F32), state, layer, layer, tiles16, tiles16,
             grad, grad, slices, slices, pltpu.VMEM((others, size // PLANE, size), F32),
-            dma((4,)), one, dma((PLANE,)), one, one, one, one, one, one, *[one] * 10,
+            dma((4,)), one, dma((3 * PLANE,)), one, one, one, one, one, one, *[one] * 10,
         ],
         compiler_params=pltpu.CompilerParams(vmem_limit_bytes=VMEM_LIMIT, collective_id=0, has_side_effects=True),
     )(*(array.reshape(flat) for array in (queries, keys, values, target)), map_q.T, map_k.T)

time: 105 us -> 82.7 us (0.79)
  Pallas kernels: 101 us -> 79.1 us
    pallas_call x1, Pallas kernels: 101 us -> 79.1 us  [per_device(): pl.pallas_call(functools.partial(kernel, heads, total_tokens), out_shape=...]
where the time goes in v5:
time: 82.7 us; the launch traced here: 82.5 us
  Pallas kernels  79.1 us (96%)
  other arithmetic  2.1 us (3%)
    pallas_call x1, Pallas kernels, per_device(): pl.pallas_call(functools.partial(kernel, heads, total_tokens), out_shape=...  79.1 us
    convert_element_type x1, other arithmetic, per_device(): hybrid = output.astype(BF16).reshape(rows, heads, size)  2.1 us

profile of v5, /device:TPU:1, one launch (start us, length us, event | category | flops | bytes accessed | tf_op | source)
XLA Modules:
  0.0 82.5 jit_solution(12408288697161502627)
XLA Ops:
  0.6 79.1 %shard_map.85 = (f32[2048,128]{1,0:T(8,128)}, f32[16,8,128]{2,1,0:T(8,128)}) custom-call(bf16[2048,128]{1,0:T(8,128)(2,1)} %bitcast.16, bf16[2048,128]{1,0:T(8,128)(2,1)} %bitcast.17, bf16[2048,128]{1,0:T(8,128)(2,1)} %bitcast.18, bf16[2048,128]{1,0:T(8,128)(2,1)} %bitcast.19, bf16[64,128]{1,0:T(8,128)(2,1)} %bitcast.20, bf16[64,128]{1,0:T(8,128)(2,1)} %bitcast.21), custom_call_target="tpu_custom_call" | custom-call | tf_op jit(solution)/shard_map/pallas_call | solution.py:533
  79.7 0.0 copy-start
  79.8 2.1 %convert_element_type.3 = bf16[2048,128]{1,0:T(8,128)(2,1)} convert(f32[2048,128]{1,0:T(8,128)} %get-tuple-element.5) | non-fusion elementwise | flops 262144 | bytes 1572864 | tf_op jit(solution)/shard_map/convert_element_type | solution.py:552
  81.9 0.0 copy-done
  81.9 0.6 slice_bitcast_fusion
Async XLA Ops:
  79.7 2.1 %copy-start = (f32[16,8,128]{2,1,0:T(8,128)S(1)}, f32[16,8,128]{2,1,0:T(8,128)}, u32[]{:S(2)}) copy-start(f32[16,8,128]{2,1,0:T(8,128)} %get-tuple-element.6) | copy-start | bytes 196612

commit v6 on v5

--- a/solution.py
+++ b/solution.py
@@ -103,60 +103,60 @@
         await_bytes(self.totals.at[pl.ds(0, self.layers - 1)], self.send)
 
 
+def groups():
+    me = lax.axis_index("seq")
+    z, x, y = me // PLANE, (me // 4) % 4, me % 4
+    low, high = x % 2, x // 2
+
+    def first(k):
+        return {"seq": (k // 2) * PLANE + (high * 2 + k % 2) * 4 + y}
+
+    def second(k):
+        return {"seq": z * PLANE + ((k % 2) * 2 + low) * 4 + k // 2}
+
+    return (z * 2 + low, first), (y * 2 + high, second)
+
+
 class Total:
-    def __init__(self, x, out, parts, totals, sems):
-        self.x, self.out, self.parts, self.totals = x, out, parts, totals
-        self.send1, self.recv1, self.send_z, self.recv_z, self.send2, self.recv2 = sems
-        me, core = lax.axis_index("seq"), lax.axis_index("head")
-        self.cores = lax.axis_size("head")
-        self.others = lax.axis_size("seq") // PLANE * self.cores
-        self.z, self.p = me // PLANE, me % PLANE
-        self.here = self.z * self.cores + core
-
-    def in_plane(self, k):
-        return {"seq": self.z * PLANE + k}
-
-    def give(self):
-        for i in range(1, PLANE):
-            to = wrapped(self.p + i, PLANE)
+    def __init__(self, grads, out, inbox, slots, sems):
+        self.grads, self.out, self.inbox, self.slots, self.sems = grads, out, inbox, slots, sems
+        self.core = lax.axis_index("head")
+
+    def swap(self):
+        other = 1 - self.core
+        return pltpu.make_async_remote_copy(
+            src_ref=self.grads.at[other], dst_ref=self.inbox, send_sem=self.sems[0], recv_sem=self.sems[1],
+            device_id={"head": other}, device_id_type=MESH,
+        )
+
+    def give(self, stage, value):
+        here, device = groups()[stage]
+        slots, send, recv = self.slots[stage], self.sems[2 + 2 * stage], self.sems[3 + 2 * stage]
+        slots[here] = value
+        for i in range(1, 8):
             pltpu.make_async_remote_copy(
-                src_ref=self.x.at[to], dst_ref=self.parts.at[self.p], send_sem=self.send1, recv_sem=self.recv1,
-                device_id=self.in_plane(to), device_id_type=MESH,
+                src_ref=slots.at[here], dst_ref=slots.at[here], send_sem=send, recv_sem=recv,
+                device_id=device(wrapped(here + i, 8)), device_id_type=MESH,
             ).start()
-        pltpu.make_async_copy(self.x.at[self.p], self.parts.at[self.p], self.recv1).start()
-
-    def collect(self):
-        await_bytes(self.parts, self.recv1)
-        self.totals[self.here] = jnp.sum(self.parts[...], 0)
-        for i in range(1, self.others):
-            at = wrapped(self.here + i, self.others)
-            pltpu.make_async_remote_copy(
-                src_ref=self.totals.at[self.here], dst_ref=self.totals.at[self.here],
-                send_sem=self.send_z, recv_sem=self.recv_z,
-                device_id={"seq": (at // self.cores) * PLANE + self.p, "head": at % self.cores}, device_id_type=MESH,
-            ).start()
-
-    def spread(self):
-        await_bytes(self.totals.at[pl.ds(0, self.others - 1)], self.recv_z)
-        self.out[self.p] = jnp.sum(self.totals[...], 0)
-        for i in range(1, PLANE):
-            pltpu.make_async_remote_copy(
-                src_ref=self.out.at[self.p], dst_ref=self.out.at[self.p], send_sem=self.send2, recv_sem=self.recv2,
-                device_id=self.in_plane(wrapped(self.p + i, PLANE)), device_id_type=MESH,
-            ).start()
+
+    def take(self, stage):
+        slots = self.slots[stage]
+        await_bytes(slots.at[pl.ds(0, 7)], self.sems[3 + 2 * stage])
+        return jnp.sum(slots[...], 0)
+
+    def share(self):
+        return pltpu.make_async_remote_copy(
+            src_ref=self.out.at[self.core], dst_ref=self.out.at[self.core], send_sem=self.sems[6], recv_sem=self.sems[7],
+            device_id={"head": 1 - self.core}, device_id_type=MESH,
+        )
 
     def finish(self):
-        most = pl.ds(0, PLANE - 1)
-        await_bytes(self.out.at[most], self.recv2)
-        await_bytes(self.out.at[most], self.send2)
-        await_bytes(self.x.at[most], self.send1)
-        await_bytes(self.totals.at[pl.ds(0, self.others - 1)], self.send_z)
+        for stage in range(2):
+            await_bytes(self.slots[stage].at[pl.ds(0, 7)], self.sems[2 + 2 * stage])
 
 
 def greet():
     me, core = lax.axis_index("seq"), lax.axis_index("head")
-    count, cores = lax.axis_size("seq"), lax.axis_size("head")
-    others = count // PLANE * cores
     z, p = me // PLANE, me % PLANE
     barrier = pltpu.get_barrier_semaphore()
 
@@ -165,23 +165,20 @@
         pl.semaphore_signal(barrier, inc=1, device_id=device, device_id_type=MESH)
         return carry
 
-    def beyond(i, carry):
-        at = (z * cores + core + i) % others
-        device = {"seq": (at // cores) * PLANE + p, "head": at % cores}
-        pl.semaphore_signal(barrier, inc=1, device_id=device, device_id_type=MESH)
-        return carry
-
     lax.fori_loop(1, PLANE, plane, 0)
-    lax.fori_loop(1, others, beyond, 0)
-    return PLANE - 1 + others - 1
+    here, device = groups()[0]
+    for i in range(1, 8):
+        pl.semaphore_signal(barrier, inc=1, device_id=device(wrapped(here + i, 8)), device_id_type=MESH)
+    pl.semaphore_signal(barrier, inc=1, device_id={"head": 1 - core}, device_id_type=MESH)
+    return PLANE - 1 + 7 + 1
 
 
 def kernel(
     heads, total_tokens, q_ref, k_ref, v_ref, t_ref, mq_ref, mk_ref, out_ref, grad_ref,
     k_in, v_in, q_in, t_in, k_wide, v_wide, q_wide, t_wide, mine, held,
     phi_all, soft_q, soft_k, numer_near, denom_near, damp, state, halo_state, d_numer_all, d_denom_all,
-    gstate, state16, state_sum, later16, later_sum, near, lead, total, totals1, totals2, out_send, out_held, gq, gk, packed, parts3, totals3,
-    load, send, recv, send_halo, recv_halo, send_lead, recv_lead, send_out, recv_out, *sems,
+    gstate, state16, state_sum, later16, later_sum, near, lead, totals1, totals2, out_send, out_held, out_wide, gq, gk, grads, inbox, slots1, slots2,
+    load, store, send, recv, send_halo, recv_halo, send_lead, recv_lead, send_out, recv_out, *sems,
 ):
     w = WINDOW
     rows = 2 * w
@@ -190,8 +187,8 @@
     greeted = greet()
     arrays = [(k_ref, k_in, k_wide), (v_ref, v_in, v_wide), (q_ref, q_in, q_wide), (t_ref, t_in, t_wide)]
     loads = [pltpu.make_async_copy(source, into, load.at[i]) for i, (source, into, wide) in enumerate(arrays)]
-    for copy in loads:
-        copy.start()
+    for j in (Q, K, V, T):
+        loads[j].start()
     me = lax.axis_index("seq")
     layers = lax.axis_size("seq") // PLANE
     z, p = me // PLANE, me % PLANE
@@ -199,7 +196,7 @@
     has_later = z < layers - 1
     forward = Across(totals1, sems[0], sems[1], False)
     backward = Across(totals2, sems[2], sems[3], True)
-    final = Total(packed, grad_ref, parts3, totals3, sems[4:10])
+    final = Total(grads, grad_ref, inbox, (slots1, slots2), sems[4:12])
 
     def in_plane(k):
         return {"seq": z * PLANE + k}
@@ -244,9 +241,10 @@
             pl.semaphore_wait(pltpu.get_barrier_semaphore(), greeted)
         lax.fori_loop(0, heads // 2, step, 0)
 
-    give((K, V), 0)
-    give((Q,), PLANE)
-    give((T,), 2 * PLANE)
+    give((Q,), 0)
+    give((K,), PLANE)
+    give((V,), 2 * PLANE)
+    give((T,), 3 * PLANE)
 
     map_q, map_k = (
         jnp.concatenate([ref[...], (-ref[...].astype(F32)).astype(BF16)], 0) for ref in (mq_ref, mk_ref)
@@ -254,7 +252,7 @@
     row = lax.broadcasted_iota(jnp.int32, (w, rows), 0)
     col = lax.broadcasted_iota(jnp.int32, (w, rows), 1)
     scale = 128 ** (-0.5)
-    total[...] = jnp.zeros_like(total)
+    zero_state = jnp.zeros((ROWS, 128), F32)
 
     def masks(c, half):
         in_window = (col > row) & (col <= row + w)
@@ -270,55 +268,69 @@
     def arriving(i):
         return wrapped(p + PLANE - 2 * i, PLANE), wrapped(p + PLANE - 2 * i - 1, PLANE)
 
+    def query_part(i, carry):
+        pair = arriving(i)
+        for c in pair:
+            await_bytes(held.at[c + 1, pl.ds(Q, 1)], recv.at[c])
+        for c in pair:
+            soft_q[c] = features(held[c + 1, Q], map_q)
+        return carry
+
     def key_part(i, carry):
         pair = arriving(i)
         for c in pair:
-            await_bytes(held.at[c + 1, pl.ds(K, 2)], recv.at[c])
+            await_bytes(held.at[c + 1, pl.ds(K, 1)], recv.at[PLANE + c])
+        for c in pair:
+            soft = features(held[c + 1, K], map_k)
+            soft_k[c] = soft
+            phi_all[c + 1] = soft.astype(BF16)
+        return carry
+
+    def state_part(i, carry):
+        pair = arriving(i)
+        for c in pair:
+            await_bytes(held.at[c + 1, pl.ds(V, 1)], recv.at[2 * PLANE + c])
 
             @pl.when((c == chunks - 1) & has_later)
             def _():
                 halo_copy.start()
 
         for c in pair:
-            soft = features(held[c + 1, K], map_k)
-            soft_k[c] = soft
-            phi = soft.astype(BF16)
-            phi_all[c + 1] = phi
-            v = held[c + 1, V]
+            phi = phi_all[c + 1]
             for half in range(2):
                 part = phi[half * w : (half + 1) * w]
-                block_state = dot_tn(part, v[half * w : (half + 1) * w])
                 block_sum = jnp.sum(part.astype(F32), 0, keepdims=True)
-                state[2 * c + half, :128, :] = block_state
+                state[2 * c + half, :128, :] = dot_tn(part, held[c + 1, V, half * w : (half + 1) * w, :])
                 state[2 * c + half, 128:, :] = jnp.broadcast_to(block_sum, (ROWS - 128, 128))
-                total[:128, :] += block_state
-                total[128:, :] += block_sum
-        return carry
-
+        return carry
+
+    def sum_of(ref):
+        return lax.fori_loop(0, chunks, lambda i, whole: whole + (ref[2 * i] + ref[2 * i + 1]), zero_state)
+
+    lax.fori_loop(0, chunks // 2, query_part, 0)
     lax.fori_loop(0, chunks // 2, key_part, 0)
-    forward.give(total[...])
-
-    @pl.when(has_prior)
-    def _():
-        await_bytes(halo_there, recv_halo)
-
-    @pl.when(jnp.logical_not(has_prior))
-    def _():
-        held[0, :2, w:, :] = jnp.zeros((2, w, 128), BF16)
-
-    phi_halo = jnp.where(has_prior, features(held[0, K, w:, :], map_k), 0.0).astype(BF16)
-    phi_all[0, w:, :] = phi_halo
-    halo_state[:128, :] = dot_tn(phi_halo, held[0, V, w:, :])
-    halo_state[128:, :] = jnp.broadcast_to(jnp.sum(phi_halo.astype(F32), 0, keepdims=True), (ROWS - 128, 128))
+    lax.fori_loop(0, chunks // 2, state_part, 0)
+    forward.give(sum_of(state))
 
     def near_part(i, carry):
-        pair = arriving(i)
-        for c in pair:
-            await_bytes(held.at[c + 1, pl.ds(Q, 1)], recv.at[PLANE + c])
-        for c in pair:
-            soft = features(held[c + 1, Q], map_q)
-            soft_q[c] = soft
-            phi_q = soft.astype(BF16)
+        @pl.when(i == chunks // 2 - 1)
+        def _():
+            @pl.when(has_prior)
+            def _():
+                await_bytes(halo_there, recv_halo)
+
+            @pl.when(jnp.logical_not(has_prior))
+            def _():
+                held[0, :2, w:, :] = jnp.zeros((2, w, 128), BF16)
+
+            phi_halo = jnp.where(has_prior, features(held[0, K, w:, :], map_k), 0.0).astype(BF16)
+            phi_all[0, w:, :] = phi_halo
+            halo_state[:128, :] = dot_tn(phi_halo, held[0, V, w:, :])
+            halo_sum = jnp.sum(phi_halo.astype(F32), 0, keepdims=True)
+            halo_state[128:, :] = jnp.broadcast_to(halo_sum, (ROWS - 128, 128))
+
+        for c in (chunks - 1 - 2 * i, chunks - 2 - 2 * i):
+            phi_q = soft_q[c].astype(BF16)
             for half in range(2):
                 block, span = pl.ds(half * w, w), slice(half * w, (half + 1) * w)
                 if half:
@@ -353,12 +365,11 @@
         return after, after + own
 
     lax.fori_loop(0, 2 * chunks, lead_states, (base - halo_state[...], base))
-    total[...] = jnp.zeros_like(total)
 
     def middle_part(i, carry):
         pair = arriving(i)
         for c in pair:
-            await_bytes(held.at[c + 1, pl.ds(T, 1)], recv.at[2 * PLANE + c])
+            await_bytes(held.at[c + 1, pl.ds(T, 1)], recv.at[3 * PLANE + c])
         for c in pair:
             phi_q = soft_q[c].astype(BF16)
             target = held[c + 1, T].astype(F32)
@@ -382,12 +393,10 @@
                 g_sum = jnp.sum(damping * d_denom * wide_pq, 0, keepdims=True)
                 gstate[b, :128, :] = g_state
                 gstate[b, 128:, :] = jnp.broadcast_to(g_sum, (ROWS - 128, 128))
-                total[:128, :] += g_state
-                total[128:, :] += g_sum
         return carry
 
     lax.fori_loop(0, chunks // 2, middle_part, 0)
-    backward.give(total[...])
+    backward.give(sum_of(gstate))
 
     def give_out(i, carry):
         c = wrapped(p + i, PLANE)
@@ -476,20 +485,26 @@
         return carry
 
     lax.fori_loop(0, chunks // 2, last_part, 0)
-    for k in range(PLANE):
-        source = gq if k < PLANE // 2 else gk
-        packed[k] = source[k % (PLANE // 2) * 8 : k % (PLANE // 2) * 8 + 8, :]
-    final.give()
+    grads[0] = gq[:FEAT, :]
+    grads[1] = gk[:FEAT, :]
+    swap = final.swap()
+    swap.start()
+    swap.wait()
+    final.give(0, grads[final.core] + inbox[...])
     await_bytes(out_held, recv_out)
 
     def arrange(i, carry):
         for head in (2 * i, 2 * i + 1):
-            out_ref[pl.ds(head, rows, stride=heads), :] = out_held[head].astype(F32)
+            out_wide[pl.ds(head, rows, stride=heads), :] = out_held[head].astype(F32)
         return carry
 
     lax.fori_loop(0, heads // 2, arrange, 0)
-    final.collect()
-    final.spread()
+    out_copy = pltpu.make_async_copy(out_wide, out_ref, store)
+    out_copy.start()
+    final.give(1, final.take(0))
+    grad_ref[final.core] = final.take(1)
+    share = final.share()
+    share.start()
     most = pl.ds(0, PLANE - 1)
     await_bytes(mine.at[most], send)
     await_bytes(out_send.at[most], send_out)
@@ -505,13 +520,14 @@
         lead_copy.wait_send()
 
     final.finish()
+    out_copy.wait()
+    share.wait()
 
 
 def per_device(queries, keys, values, target, map_q, map_k):
     rows, heads, size = queries.shape
     total_tokens = rows * lax.axis_size("seq")
     layers = lax.axis_size("seq") // PLANE
-    others = layers * lax.axis_size("head")
     chunks = PLANE
     flat = (rows * heads, size)
     wide = pltpu.VMEM(flat, F32)
@@ -525,7 +541,7 @@
     state_sums = pltpu.VMEM((2 * chunks, ROWS - 128, size), F32)
     layer = pltpu.VMEM((layers, ROWS, size), F32)
     grad = pltpu.VMEM((size, size), F32)
-    slices = pltpu.VMEM((PLANE, size // PLANE, size), F32)
+    slots = pltpu.VMEM((8, FEAT, size), F32)
     dma = pltpu.SemaphoreType.DMA
     one = dma(())
     vmem = pl.BlockSpec(memory_space=pltpu.VMEM)
@@ -534,24 +550,23 @@
         functools.partial(kernel, heads, total_tokens),
         out_shape=[
             jax.ShapeDtypeStruct(flat, F32),
-            jax.ShapeDtypeStruct((PLANE, size // PLANE, size), F32),
+            jax.ShapeDtypeStruct((2, FEAT, size), F32),
         ],
         in_specs=[hbm] * 4 + [vmem] * 2,
-        out_specs=[vmem] * 2,
+        out_specs=[hbm, vmem],
         scratch_shapes=[
             narrow, narrow, narrow, narrow, wide, wide, wide, wide,
             pltpu.VMEM((heads, 4, rows, size), BF16), pltpu.VMEM((chunks + 1, 4, rows, size), BF16),
             pltpu.VMEM((chunks + 1, rows, size), BF16), tiles, tiles, tiles, column, column, states, state, tiles, column,
             states, split_states, state_sums, split_states, state_sums, tiles,
-            pltpu.VMEM((chunks + 1, WINDOW, size), F32), state, layer, layer, tiles16, tiles16,
-            grad, grad, slices, slices, pltpu.VMEM((others, size // PLANE, size), F32),
-            dma((4,)), one, dma((3 * PLANE,)), one, one, one, one, one, one, *[one] * 10,
+            pltpu.VMEM((chunks + 1, WINDOW, size), F32), layer, layer, tiles16, tiles16, wide,
+            grad, grad, pltpu.VMEM((2, FEAT, size), F32), pltpu.VMEM((FEAT, size), F32), slots, slots,
+            dma((4,)), one, one, dma((4 * PLANE,)), one, one, one, one, one, one, *[one] * 12,
         ],
         compiler_params=pltpu.CompilerParams(vmem_limit_bytes=VMEM_LIMIT, collective_id=0, has_side_effects=True),
     )(*(array.reshape(flat) for array in (queries, keys, values, target)), map_q.T, map_k.T)
     hybrid = output.astype(BF16).reshape(rows, heads, size)
-    grads = grads.reshape(size, size)
-    return hybrid, grads[:FEAT].T, grads[FEAT:].T
+    return hybrid, grads[0].T, grads[1].T
 
 
 def solution(mesh):

time: 82.7 us -> 77.8 us (0.941)
  Pallas kernels: 79.1 us -> 74.2 us
    pallas_call x1, Pallas kernels: 79.1 us -> 74.2 us  [per_device(): pl.pallas_call(functools.partial(kernel, heads, total_tokens), out_shape=...]
where the time goes in v6:
time: 77.8 us; the launch traced here: 77.6 us
  Pallas kernels  74.2 us (95%)
  other arithmetic  2.1 us (3%)
    pallas_call x1, Pallas kernels, per_device(): pl.pallas_call(functools.partial(kernel, heads, total_tokens), out_shape=...  74.2 us
    convert_element_type x1, other arithmetic, per_device(): hybrid = output.astype(BF16).reshape(rows, heads, size)  2.1 us

profile of v6, /device:TPU:1, one launch (start us, length us, event | category | flops | bytes accessed | tf_op | source)
XLA Modules:
  0.0 77.6 jit_solution(4368323875553374416)
XLA Ops:
  0.6 74.2 %shard_map.85 = (f32[2048,128]{1,0:T(8,128)}, f32[2,64,128]{2,1,0:T(8,128)}) custom-call(bf16[2048,128]{1,0:T(8,128)(2,1)} %bitcast.16, bf16[2048,128]{1,0:T(8,128)(2,1)} %bitcast.17, bf16[2048,128]{1,0:T(8,128)(2,1)} %bitcast.18, bf16[2048,128]{1,0:T(8,128)(2,1)} %bitcast.19, bf16[64,128]{1,0:T(8,128)(2,1)} %bitcast.20, bf16[64,128]{1,0:T(8,128)(2,1)} %bitcast.21), custom_call_target="tpu_custom_call" | custom-call | tf_op jit(solution)/shard_map/pallas_call | solution.py:549
  74.8 0.0 copy-start
  74.8 2.1 %convert_element_type.3 = bf16[2048,128]{1,0:T(8,128)(2,1)} convert(f32[2048,128]{1,0:T(8,128)} %get-tuple-element.5) | non-fusion elementwise | flops 262144 | bytes 1572864 | tf_op jit(solution)/shard_map/convert_element_type | solution.py:568
  76.9 0.0 copy-done
  76.9 0.6 slice_bitcast_fusion
Async XLA Ops:
  74.8 2.1 %copy-start = (f32[2,64,128]{2,1,0:T(8,128)S(1)}, f32[2,64,128]{2,1,0:T(8,128)}, u32[]{:S(2)}) copy-start(f32[2,64,128]{2,1,0:T(8,128)} %get-tuple-element.6) | copy-start | bytes 196612

commit v7 on v6

--- a/solution.py
+++ b/solution.py
@@ -176,7 +176,7 @@
 def kernel(
     heads, total_tokens, q_ref, k_ref, v_ref, t_ref, mq_ref, mk_ref, out_ref, grad_ref,
     k_in, v_in, q_in, t_in, k_wide, v_wide, q_wide, t_wide, mine, held,
-    phi_all, soft_q, soft_k, numer_near, denom_near, damp, state, halo_state, d_numer_all, d_denom_all,
+    phi_all, soft_q, soft_k, weights, numer_near, denom_near, damp, state, halo_state, d_numer_all, d_denom_all,
     gstate, state16, state_sum, later16, later_sum, near, lead, totals1, totals2, out_send, out_held, out_wide, gq, gk, grads, inbox, slots1, slots2,
     load, store, send, recv, send_halo, recv_halo, send_lead, recv_lead, send_out, recv_out, *sems,
 ):
@@ -201,11 +201,30 @@
     def in_plane(k):
         return {"seq": z * PLANE + k}
 
-    halo_there = held.at[0, pl.ds(0, 2), pl.ds(w, w)]
-    halo_copy = pltpu.make_async_remote_copy(
-        src_ref=held.at[chunks, pl.ds(0, 2), pl.ds(w, w)], dst_ref=halo_there, send_sem=send_halo, recv_sem=recv_halo,
-        device_id={"seq": jnp.where(has_later, z + 1, 0) * PLANE + p}, device_id_type=MESH,
-    )
+    def halo_there(j):
+        return held.at[0, pl.ds(j, 1), pl.ds(w, w)]
+
+    def halo_copy(j):
+        return pltpu.make_async_remote_copy(
+            src_ref=held.at[chunks, pl.ds(j, 1), pl.ds(w, w)], dst_ref=halo_there(j),
+            send_sem=send_halo.at[j], recv_sem=recv_halo.at[j],
+            device_id={"seq": jnp.where(has_later, z + 1, 0) * PLANE + p}, device_id_type=MESH,
+        )
+
+    def give_halo(j, c):
+        @pl.when((c == chunks - 1) & has_later)
+        def _():
+            halo_copy(j).start()
+
+    def take_halo(j):
+        @pl.when(has_prior)
+        def _():
+            await_bytes(halo_there(j), recv_halo.at[j])
+
+        @pl.when(jnp.logical_not(has_prior))
+        def _():
+            held[0, j, w:, :] = jnp.zeros((w, 128), BF16)
+
     lead_copy = pltpu.make_async_remote_copy(
         src_ref=lead.at[0], dst_ref=lead.at[chunks], send_sem=send_lead, recv_sem=recv_lead,
         device_id={"seq": jnp.where(has_prior, z - 1, layers - 1) * PLANE + p}, device_id_type=MESH,
@@ -280,6 +299,7 @@
         pair = arriving(i)
         for c in pair:
             await_bytes(held.at[c + 1, pl.ds(K, 1)], recv.at[PLANE + c])
+            give_halo(K, c)
         for c in pair:
             soft = features(held[c + 1, K], map_k)
             soft_k[c] = soft
@@ -290,10 +310,7 @@
         pair = arriving(i)
         for c in pair:
             await_bytes(held.at[c + 1, pl.ds(V, 1)], recv.at[2 * PLANE + c])
-
-            @pl.when((c == chunks - 1) & has_later)
-            def _():
-                halo_copy.start()
+            give_halo(V, c)
 
         for c in pair:
             phi = phi_all[c + 1]
@@ -309,45 +326,49 @@
 
     lax.fori_loop(0, chunks // 2, query_part, 0)
     lax.fori_loop(0, chunks // 2, key_part, 0)
-    lax.fori_loop(0, chunks // 2, state_part, 0)
-    forward.give(sum_of(state))
-
-    def near_part(i, carry):
+
+    def weight_part(i, carry):
         @pl.when(i == chunks // 2 - 1)
         def _():
-            @pl.when(has_prior)
-            def _():
-                await_bytes(halo_there, recv_halo)
-
-            @pl.when(jnp.logical_not(has_prior))
-            def _():
-                held[0, :2, w:, :] = jnp.zeros((2, w, 128), BF16)
-
-            phi_halo = jnp.where(has_prior, features(held[0, K, w:, :], map_k), 0.0).astype(BF16)
-            phi_all[0, w:, :] = phi_halo
-            halo_state[:128, :] = dot_tn(phi_halo, held[0, V, w:, :])
-            halo_sum = jnp.sum(phi_halo.astype(F32), 0, keepdims=True)
-            halo_state[128:, :] = jnp.broadcast_to(halo_sum, (ROWS - 128, 128))
+            take_halo(K)
+            phi_all[0, w:, :] = jnp.where(has_prior, features(held[0, K, w:, :], map_k), 0.0).astype(BF16)
 
         for c in (chunks - 1 - 2 * i, chunks - 2 - 2 * i):
             phi_q = soft_q[c].astype(BF16)
             for half in range(2):
                 block, span = pl.ds(half * w, w), slice(half * w, (half + 1) * w)
                 if half:
-                    kn, vn, pn = held[c + 1, K], held[c + 1, V], phi_all[c + 1]
+                    kn, pn = held[c + 1, K], phi_all[c + 1]
                 else:
-                    kn, vn, pn = ext(held.at[:, K], c), ext(held.at[:, V], c), ext(phi_all, c)
+                    kn, pn = ext(held.at[:, K], c), ext(phi_all, c)
                 in_window, in_far = masks(c, half)
                 scores = jnp.where(in_window, dot_nt(held[c + 1, Q, span, :], kn) * scale, -jnp.inf)
                 top = jnp.max(scores, -1, keepdims=True)
                 damping = jnp.exp(-top)
                 far = damping * dot_nt(phi_q[span], pn)
                 weight = jnp.exp(scores - top) + jnp.where(in_far, far, 0.0)
-                numer_near[c, block, :] = dot_nn(weight.astype(BF16), vn)
+                weights[c, block, :] = weight.astype(BF16)
                 denom_near[c, block, :] = jnp.sum(weight, -1, keepdims=True)
                 damp[c, block, :] = damping
         return carry
 
+    def near_part(i, carry):
+        @pl.when(i == chunks // 2 - 1)
+        def _():
+            take_halo(V)
+            phi_halo = phi_all[0, w:, :]
+            halo_state[:128, :] = dot_tn(phi_halo, held[0, V, w:, :])
+            halo_sum = jnp.sum(phi_halo.astype(F32), 0, keepdims=True)
+            halo_state[128:, :] = jnp.broadcast_to(halo_sum, (ROWS - 128, 128))
+
+        for c in (chunks - 1 - 2 * i, chunks - 2 - 2 * i):
+            numer_near[c, :w, :] = dot_nn(weights[c, :w, :], ext(held.at[:, V], c))
+            numer_near[c, w:, :] = dot_nn(weights[c, w:, :], held[c + 1, V])
+        return carry
+
+    lax.fori_loop(0, chunks // 2, weight_part, 0)
+    lax.fori_loop(0, chunks // 2, state_part, 0)
+    forward.give(sum_of(state))
     lax.fori_loop(0, chunks // 2, near_part, 0)
 
     def store_split(into, sums, b, whole):
@@ -513,7 +534,8 @@
 
     @pl.when(has_later)
     def _():
-        halo_copy.wait_send()
+        halo_copy(K).wait_send()
+        halo_copy(V).wait_send()
 
     @pl.when(has_prior)
     def _():
@@ -557,11 +579,11 @@
         scratch_shapes=[
             narrow, narrow, narrow, narrow, wide, wide, wide, wide,
             pltpu.VMEM((heads, 4, rows, size), BF16), pltpu.VMEM((chunks + 1, 4, rows, size), BF16),
-            pltpu.VMEM((chunks + 1, rows, size), BF16), tiles, tiles, tiles, column, column, states, state, tiles, column,
+            pltpu.VMEM((chunks + 1, rows, size), BF16), tiles, tiles, tiles16, tiles, column, column, states, state, tiles, column,
             states, split_states, state_sums, split_states, state_sums, tiles,
             pltpu.VMEM((chunks + 1, WINDOW, size), F32), layer, layer, tiles16, tiles16, wide,
             grad, grad, pltpu.VMEM((2, FEAT, size), F32), pltpu.VMEM((FEAT, size), F32), slots, slots,
-            dma((4,)), one, one, dma((4 * PLANE,)), one, one, one, one, one, one, *[one] * 12,
+            dma((4,)), one, one, dma((4 * PLANE,)), dma((2,)), dma((2,)), one, one, one, one, *[one] * 12,
         ],
         compiler_params=pltpu.CompilerParams(vmem_limit_bytes=VMEM_LIMIT, collective_id=0, has_side_effects=True),
     )(*(array.reshape(flat) for array in (queries, keys, values, target)), map_q.T, map_k.T)

time: 77.8 us -> 78.7 us (1.012)
  Pallas kernels: 74.2 us -> 75 us
    pallas_call x1, Pallas kernels: 74.2 us -> 75 us  [per_device(): pl.pallas_call(functools.partial(kernel, heads, total_tokens), out_shape=...]
where the time goes in v7:
time: 78.7 us; the launch traced here: 78.4 us
  Pallas kernels  75 us (95%)
  other arithmetic  2.1 us (3%)
    pallas_call x1, Pallas kernels, per_device(): pl.pallas_call(functools.partial(kernel, heads, total_tokens), out_shape=...  75 us
    convert_element_type x1, other arithmetic, per_device(): hybrid = output.astype(BF16).reshape(rows, heads, size)  2.1 us

profile of v7, /device:TPU:1, one launch (start us, length us, event | category | flops | bytes accessed | tf_op | source)
XLA Modules:
  0.0 78.4 jit_solution(10365639873123618815)
XLA Ops:
  0.6 75.0 %shard_map.85 = (f32[2048,128]{1,0:T(8,128)}, f32[2,64,128]{2,1,0:T(8,128)}) custom-call(bf16[2048,128]{1,0:T(8,128)(2,1)} %bitcast.16, bf16[2048,128]{1,0:T(8,128)(2,1)} %bitcast.17, bf16[2048,128]{1,0:T(8,128)(2,1)} %bitcast.18, bf16[2048,128]{1,0:T(8,128)(2,1)} %bitcast.19, bf16[64,128]{1,0:T(8,128)(2,1)} %bitcast.20, bf16[64,128]{1,0:T(8,128)(2,1)} %bitcast.21), custom_call_target="tpu_custom_call" | custom-call | tf_op jit(solution)/shard_map/pallas_call | solution.py:571
  75.7 0.0 copy-start
  75.7 2.1 %convert_element_type.3 = bf16[2048,128]{1,0:T(8,128)(2,1)} convert(f32[2048,128]{1,0:T(8,128)} %get-tuple-element.5) | non-fusion elementwise | flops 262144 | bytes 1572864 | tf_op jit(solution)/shard_map/convert_element_type | solution.py:590
  77.8 0.0 copy-done
  77.8 0.6 slice_bitcast_fusion
Async XLA Ops:
  75.7 2.1 %copy-start = (f32[2,64,128]{2,1,0:T(8,128)S(1)}, f32[2,64,128]{2,1,0:T(8,128)}, u32[]{:S(2)}) copy-start(f32[2,64,128]{2,1,0:T(8,128)} %get-tuple-element.6) | copy-start | bytes 196612

commit v8 on v7

--- a/solution.py
+++ b/solution.py
@@ -388,12 +388,8 @@
     lax.fori_loop(0, 2 * chunks, lead_states, (base - halo_state[...], base))
 
     def middle_part(i, carry):
-        pair = arriving(i)
-        for c in pair:
-            await_bytes(held.at[c + 1, pl.ds(T, 1)], recv.at[3 * PLANE + c])
-        for c in pair:
+        for c in arriving(i):
             phi_q = soft_q[c].astype(BF16)
-            target = held[c + 1, T].astype(F32)
             for half in range(2):
                 block, span, b = pl.ds(half * w, w), slice(half * w, (half + 1) * w), 2 * c + half
                 pq = phi_q[span]
@@ -405,6 +401,23 @@
                 inverse = 1.0 / (denom_near[c, block, :] + damping * state_den)
                 output = numer * inverse
                 out_send[c, block, :] = output.astype(BF16)
+                numer_near[c, block, :] = output
+                denom_near[c, block, :] = inverse
+        return carry
+
+    def grad_part(i, carry):
+        pair = arriving(i)
+        for c in pair:
+            await_bytes(held.at[c + 1, pl.ds(T, 1)], recv.at[3 * PLANE + c])
+        for c in pair:
+            phi_q = soft_q[c].astype(BF16)
+            target = held[c + 1, T].astype(F32)
+            for half in range(2):
+                block, span, b = pl.ds(half * w, w), slice(half * w, (half + 1) * w), 2 * c + half
+                pq = phi_q[span]
+                wide_pq = pq.astype(F32)
+                damping = damp[c, block, :]
+                output, inverse = numer_near[c, block, :], denom_near[c, block, :]
                 d_out = (output - target[span]) * (2.0 / total_tokens)
                 d_numer = d_out * inverse
                 d_denom = -jnp.sum(d_out * output, -1, keepdims=True) * inverse
@@ -417,6 +430,7 @@
         return carry
 
     lax.fori_loop(0, chunks // 2, middle_part, 0)
+    lax.fori_loop(0, chunks // 2, grad_part, 0)
     backward.give(sum_of(gstate))
 
     def give_out(i, carry):

time: 78.7 us -> 79.9 us (1.015)
  Pallas kernels: 75 us -> 76.3 us
    pallas_call x1, Pallas kernels: 75 us -> 76.3 us  [per_device(): pl.pallas_call(functools.partial(kernel, heads, total_tokens), out_shape=...]
where the time goes in v8:
time: 79.9 us; the launch traced here: 79.7 us
  Pallas kernels  76.3 us (95%)
  other arithmetic  2.1 us (3%)
    pallas_call x1, Pallas kernels, per_device(): pl.pallas_call(functools.partial(kernel, heads, total_tokens), out_shape=...  76.3 us
    convert_element_type x1, other arithmetic, per_device(): hybrid = output.astype(BF16).reshape(rows, heads, size)  2.1 us

profile of v8, /device:TPU:1, one launch (start us, length us, event | category | flops | bytes accessed | tf_op | source)
XLA Modules:
  0.0 79.7 jit_solution(4932118327974617882)
XLA Ops:
  0.6 76.3 %shard_map.85 = (f32[2048,128]{1,0:T(8,128)}, f32[2,64,128]{2,1,0:T(8,128)}) custom-call(bf16[2048,128]{1,0:T(8,128)(2,1)} %bitcast.16, bf16[2048,128]{1,0:T(8,128)(2,1)} %bitcast.17, bf16[2048,128]{1,0:T(8,128)(2,1)} %bitcast.18, bf16[2048,128]{1,0:T(8,128)(2,1)} %bitcast.19, bf16[64,128]{1,0:T(8,128)(2,1)} %bitcast.20, bf16[64,128]{1,0:T(8,128)(2,1)} %bitcast.21), custom_call_target="tpu_custom_call" | custom-call | tf_op jit(solution)/shard_map/pallas_call | solution.py:585
  76.9 0.0 copy-start
  76.9 2.1 %convert_element_type.3 = bf16[2048,128]{1,0:T(8,128)(2,1)} convert(f32[2048,128]{1,0:T(8,128)} %get-tuple-element.5) | non-fusion elementwise | flops 262144 | bytes 1572864 | tf_op jit(solution)/shard_map/convert_element_type | solution.py:604
  79.0 0.0 copy-done
  79.0 0.6 slice_bitcast_fusion
Async XLA Ops:
  76.9 2.1 %copy-start = (f32[2,64,128]{2,1,0:T(8,128)S(1)}, f32[2,64,128]{2,1,0:T(8,128)}, u32[]{:S(2)}) copy-start(f32[2,64,128]{2,1,0:T(8,128)} %get-tuple-element.6) | copy-start | bytes 196612

commit v9 on v6

--- a/solution.py
+++ b/solution.py
@@ -242,9 +242,8 @@
         lax.fori_loop(0, heads // 2, step, 0)
 
     give((Q,), 0)
-    give((K,), PLANE)
-    give((V,), 2 * PLANE)
-    give((T,), 3 * PLANE)
+    give((K, V), PLANE)
+    give((T,), 2 * PLANE)
 
     map_q, map_k = (
         jnp.concatenate([ref[...], (-ref[...].astype(F32)).astype(BF16)], 0) for ref in (mq_ref, mk_ref)
@@ -279,7 +278,12 @@
     def key_part(i, carry):
         pair = arriving(i)
         for c in pair:
-            await_bytes(held.at[c + 1, pl.ds(K, 1)], recv.at[PLANE + c])
+            await_bytes(held.at[c + 1, pl.ds(K, 2)], recv.at[PLANE + c])
+
+            @pl.when((c == chunks - 1) & has_later)
+            def _():
+                halo_copy.start()
+
         for c in pair:
             soft = features(held[c + 1, K], map_k)
             soft_k[c] = soft
@@ -287,15 +291,7 @@
         return carry
 
     def state_part(i, carry):
-        pair = arriving(i)
-        for c in pair:
-            await_bytes(held.at[c + 1, pl.ds(V, 1)], recv.at[2 * PLANE + c])
-
-            @pl.when((c == chunks - 1) & has_later)
-            def _():
-                halo_copy.start()
-
-        for c in pair:
+        for c in arriving(i):
             phi = phi_all[c + 1]
             for half in range(2):
                 part = phi[half * w : (half + 1) * w]
@@ -369,7 +365,7 @@
     def middle_part(i, carry):
         pair = arriving(i)
         for c in pair:
-            await_bytes(held.at[c + 1, pl.ds(T, 1)], recv.at[3 * PLANE + c])
+            await_bytes(held.at[c + 1, pl.ds(T, 1)], recv.at[2 * PLANE + c])
         for c in pair:
             phi_q = soft_q[c].astype(BF16)
             target = held[c + 1, T].astype(F32)
@@ -561,7 +557,7 @@
             states, split_states, state_sums, split_states, state_sums, tiles,
             pltpu.VMEM((chunks + 1, WINDOW, size), F32), layer, layer, tiles16, tiles16, wide,
             grad, grad, pltpu.VMEM((2, FEAT, size), F32), pltpu.VMEM((FEAT, size), F32), slots, slots,
-            dma((4,)), one, one, dma((4 * PLANE,)), one, one, one, one, one, one, *[one] * 12,
+            dma((4,)), one, one, dma((3 * PLANE,)), one, one, one, one, one, one, *[one] * 12,
         ],
         compiler_params=pltpu.CompilerParams(vmem_limit_bytes=VMEM_LIMIT, collective_id=0, has_side_effects=True),
     )(*(array.reshape(flat) for array in (queries, keys, values, target)), map_q.T, map_k.T)

time: 77.8 us -> 81.6 us (1.049)
  Pallas kernels: 74.2 us -> 78 us
    pallas_call x1, Pallas kernels: 74.2 us -> 78 us  [per_device(): pl.pallas_call(functools.partial(kernel, heads, total_tokens), out_shape=...]
where the time goes in v9:
time: 81.6 us; the launch traced here: 81.4 us
  Pallas kernels  78 us (96%)
  other arithmetic  2.1 us (3%)
    pallas_call x1, Pallas kernels, per_device(): pl.pallas_call(functools.partial(kernel, heads, total_tokens), out_shape=...  78 us
    convert_element_type x1, other arithmetic, per_device(): hybrid = output.astype(BF16).reshape(rows, heads, size)  2.1 us

profile of v9, /device:TPU:1, one launch (start us, length us, event | category | flops | bytes accessed | tf_op | source)
XLA Modules:
  0.0 81.4 jit_solution(4747383677654313689)
XLA Ops:
  0.6 78.0 %shard_map.85 = (f32[2048,128]{1,0:T(8,128)}, f32[2,64,128]{2,1,0:T(8,128)}) custom-call(bf16[2048,128]{1,0:T(8,128)(2,1)} %bitcast.16, bf16[2048,128]{1,0:T(8,128)(2,1)} %bitcast.17, bf16[2048,128]{1,0:T(8,128)(2,1)} %bitcast.18, bf16[2048,128]{1,0:T(8,128)(2,1)} %bitcast.19, bf16[64,128]{1,0:T(8,128)(2,1)} %bitcast.20, bf16[64,128]{1,0:T(8,128)(2,1)} %bitcast.21), custom_call_target="tpu_custom_call" | custom-call | tf_op jit(solution)/shard_map/pallas_call | solution.py:545
  78.6 0.0 copy-start
  78.7 2.1 %convert_element_type.3 = bf16[2048,128]{1,0:T(8,128)(2,1)} convert(f32[2048,128]{1,0:T(8,128)} %get-tuple-element.5) | non-fusion elementwise | flops 262144 | bytes 1572864 | tf_op jit(solution)/shard_map/convert_element_type | solution.py:564
  80.8 0.0 copy-done
  80.8 0.6 slice_bitcast_fusion
Async XLA Ops:
  78.6 2.1 %copy-start = (f32[2,64,128]{2,1,0:T(8,128)S(1)}, f32[2,64,128]{2,1,0:T(8,128)}, u32[]{:S(2)}) copy-start(f32[2,64,128]{2,1,0:T(8,128)} %get-tuple-element.6) | copy-start | bytes 196612

commit v10 on v6

--- a/solution.py
+++ b/solution.py
@@ -244,7 +244,6 @@
     give((Q,), 0)
     give((K,), PLANE)
     give((V,), 2 * PLANE)
-    give((T,), 3 * PLANE)
 
     map_q, map_k = (
         jnp.concatenate([ref[...], (-ref[...].astype(F32)).astype(BF16)], 0) for ref in (mq_ref, mk_ref)
@@ -308,6 +307,7 @@
         return lax.fori_loop(0, chunks, lambda i, whole: whole + (ref[2 * i] + ref[2 * i + 1]), zero_state)
 
     lax.fori_loop(0, chunks // 2, query_part, 0)
+    give((T,), 3 * PLANE)
     lax.fori_loop(0, chunks // 2, key_part, 0)
     lax.fori_loop(0, chunks // 2, state_part, 0)
     forward.give(sum_of(state))

time: 77.8 us -> 77.8 us (level)
  no operation moved by 1% of the time
where the time goes in v10:
time: 77.8 us; the launch traced here: 77.6 us
  Pallas kernels  74.2 us (95%)
  other arithmetic  2.1 us (3%)
    pallas_call x1, Pallas kernels, per_device(): pl.pallas_call(functools.partial(kernel, heads, total_tokens), out_shape=...  74.2 us
    convert_element_type x1, other arithmetic, per_device(): hybrid = output.astype(BF16).reshape(rows, heads, size)  2.1 us

profile of v10, /device:TPU:1, one launch (start us, length us, event | category | flops | bytes accessed | tf_op | source)
XLA Modules:
  0.0 77.6 jit_solution(13882932793710467252)
XLA Ops:
  0.6 74.2 %shard_map.85 = (f32[2048,128]{1,0:T(8,128)}, f32[2,64,128]{2,1,0:T(8,128)}) custom-call(bf16[2048,128]{1,0:T(8,128)(2,1)} %bitcast.16, bf16[2048,128]{1,0:T(8,128)(2,1)} %bitcast.17, bf16[2048,128]{1,0:T(8,128)(2,1)} %bitcast.18, bf16[2048,128]{1,0:T(8,128)(2,1)} %bitcast.19, bf16[64,128]{1,0:T(8,128)(2,1)} %bitcast.20, bf16[64,128]{1,0:T(8,128)(2,1)} %bitcast.21), custom_call_target="tpu_custom_call" | custom-call | tf_op jit(solution)/shard_map/pallas_call | solution.py:549
  74.8 0.0 copy-start
  74.8 2.1 %convert_element_type.3 = bf16[2048,128]{1,0:T(8,128)(2,1)} convert(f32[2048,128]{1,0:T(8,128)} %get-tuple-element.5) | non-fusion elementwise | flops 262144 | bytes 1572864 | tf_op jit(solution)/shard_map/convert_element_type | solution.py:568
  76.9 0.0 copy-done
  76.9 0.6 slice_bitcast_fusion
Async XLA Ops:
  74.8 2.1 %copy-start = (f32[2,64,128]{2,1,0:T(8,128)S(1)}, f32[2,64,128]{2,1,0:T(8,128)}, u32[]{:S(2)}) copy-start(f32[2,64,128]{2,1,0:T(8,128)} %get-tuple-element.6) | copy-start | bytes 196612
